TPU v7x, 256 devices: a whole 4x4x8 slice. The times are simulated.
256 devices in a mesh: head: 4 (over y_hi, core), ctx: 64 (over x, y_lo, z).
Axes of the slice: x: 4, y: 4 (y_hi: 2, y_lo: 2; y = y_hi * 2 + y_lo), z: 8, core: 2. Of those that a mesh axis runs over, the one named last changes fastest.
Arguments:
- q_new: bfloat16 [512, 8192], P(('head', 'ctx')), may hold values from -20 to 20
- kv_new: bfloat16 [512, 2048], P(('head', 'ctx')), may hold values from -4 to 4
- k_cache: bfloat16 [8, 131072, 128], P('head', 'ctx'), may hold values from -4 to 4
- v_cache: bfloat16 [8, 131072, 128], P('head', 'ctx'), may hold values from -4 to 4
- span_len: int32 [64], P('ctx'), may hold values from 1 to 2048, 81920 in all
- order: int32 [512], replicated, may hold values from 0 to 511, each once
Outputs:
- attended: bfloat16 [512, 8192], P(('head', 'ctx'))
Inputs may be any that keep to these rules, and one draw needn't show every extreme that they name: `span_len`: in every span at least one slot is valid, and some span is full. `order`: each position appears once.
All inputs are finite; a program needn't handle non-finite values. No bound on the sum of `span_len` on one device may be relied on, other than what follows from the above.
Results may differ from a plain program's by a relative error of at most 0.002.
Values may be sent and summed in bfloat16 or wider, within the bound.
A program may use at most 64 MiB of HBM per device.

v0:
```python
import jax
import jax.numpy as jnp
from jax import lax
from jax.sharding import PartitionSpec as P

masked = -1e30


def attend(
    q_rows, q_order, keys_cached, values_cached, keys_fresh, values_fresh, valid_slots, fresh_order
):
    rows = q_rows.shape[0]
    kv_dev, slots, width = keys_cached.shape
    group = q_rows.shape[1] // (kv_dev * width)
    scale = width ** (-0.5)
    q_four = q_rows.reshape(rows, kv_dev, group, width)
    s_cached = (
        jnp.einsum("rkgd,ksd->rkgs", q_four, keys_cached, preferred_element_type=jnp.float32)
        * scale
    )
    s_cached = jnp.where(valid_slots[None, None, None, :], s_cached, masked)
    s_fresh = (
        jnp.einsum("rkgd,tkd->rkgt", q_four, keys_fresh, preferred_element_type=jnp.float32) * scale
    )
    seen = fresh_order[None, :] <= q_order[:, None]
    s_fresh = jnp.where(seen[:, None, None, :], s_fresh, masked)
    peak = jnp.maximum(jnp.max(s_cached, -1), jnp.max(s_fresh, -1))
    p_cached = jnp.exp(s_cached - peak[..., None])
    p_fresh = jnp.exp(s_fresh - peak[..., None])
    total = jnp.sum(p_cached, -1) + jnp.sum(p_fresh, -1)
    part_out = jnp.einsum(
        "rkgs,ksd->rkgd",
        p_cached.astype(jnp.bfloat16),
        values_cached,
        preferred_element_type=jnp.float32,
    )
    part_out = part_out + jnp.einsum(
        "rkgt,tkd->rkgd",
        p_fresh.astype(jnp.bfloat16),
        values_fresh,
        preferred_element_type=jnp.float32,
    )
    return (part_out.reshape(rows, -1), peak.reshape(rows, -1), total.reshape(rows, -1))


def blocked(q_rows, q_order, context):
    rows = q_rows.shape[0]
    blocks = rows // 64
    results = lax.map(
        lambda pair: attend(pair[0], pair[1], *context),
        (q_rows.reshape(blocks, 64, -1), q_order.reshape(blocks, 64)),
    )
    return tuple((item.reshape(rows, -1) for item in results))


def shards(q_new, kv_new, k_cache, v_cache, span_len, order):
    heads_count = lax.axis_size("head")
    spans = lax.axis_size("ctx")
    my_span = lax.axis_index("ctx")
    kv_dev, slots, width = k_cache.shape
    local_rows = q_new.shape[0]
    owned = local_rows * heads_count
    q_own, kv_own = (
        lax.all_to_all(q_new, "head", split_axis=1, concat_axis=0, tiled=True),
        lax.all_to_all(kv_new, "head", split_axis=1, concat_axis=0, tiled=True),
    )
    fresh = kv_own.reshape(owned, kv_dev, 2, width)
    keys_fresh = fresh[:, :, 0, :]
    values_fresh = fresh[:, :, 1, :]
    order_grid = order.reshape(heads_count, spans, local_rows)
    fresh_order = lax.dynamic_index_in_dim(order_grid, my_span, 1, False).reshape(-1)
    gathered_order = jnp.transpose(order_grid, (1, 0, 2)).reshape(-1)
    valid_slots = jnp.arange(slots) < span_len[0]
    context = (k_cache, v_cache, keys_fresh, values_fresh, valid_slots, fresh_order)
    head_cols = q_own.shape[1]
    head_group = head_cols // width
    q_all = lax.all_gather(q_own, "ctx", axis=0, tiled=True)
    part_out, peak, total = blocked(q_all, gathered_order, context)
    got_out, got_peak, got_total = (
        lax.all_to_all(part_out[None], "ctx", split_axis=1, concat_axis=0, tiled=True),
        lax.all_to_all(peak[None], "ctx", split_axis=1, concat_axis=0, tiled=True),
        lax.all_to_all(total[None], "ctx", split_axis=1, concat_axis=0, tiled=True),
    )
    top = jnp.max(got_peak, 0)
    scaling = jnp.exp(got_peak - top[None])
    numer = jnp.sum(got_out.reshape(spans, owned, head_group, width) * scaling[..., None], 0)
    denom = jnp.sum(got_total * scaling, 0)
    result = (numer / denom[..., None]).reshape(owned, head_cols).astype(jnp.bfloat16)
    return lax.all_to_all(result, "head", split_axis=0, concat_axis=1, tiled=True)


def solution(mesh):
    return jax.shard_map(
        shards,
        mesh=mesh,
        in_specs=(
            P(("head", "ctx"), None),
            P(("head", "ctx"), None),
            P("head", "ctx", None),
            P("head", "ctx", None),
            P("ctx"),
            P(),
        ),
        out_specs=P(("head", "ctx"), None),
        check_vma=False,
    )
```

profile of v0, /device:TPU:1, one launch (start us, length us, event | category | flops | bytes accessed | tf_op | source)
XLA Modules:
  0.0 595.4 jit_solution(9157011603127615832)
XLA Ops:
  6.5 11.1 %all_to_all.87 = bf16[2,4,2048]{2,0,1:T(2,128)(2,1)S(1)} all-to-all(bf16[2,4,2048]{2,0,1:T(2,128)(2,1)} %bitcast.139), channel_id=1, replica_groups=mesh['head'=4,'ctx'=64] {'head'}, dimensions={1} | all-to-all | bytes 65536 | tf_op jit(solution)/shard_map/all_to_all | solution.py:64
  27.0 247.4 %all-gather.2.cloned.1.call-done = bf16[512,2048]{1,0:T(8,128)(2,1)} async-done(((bf16[8,2048]{1,0:T(8,128)(2,1)}), bf16[512,2048]{1,0:T(8,128)(2,1)}) %all-gather.2.cloned.1.call-update) | async-done | bytes 2097168 | tf_op jit(solution)/shard_map/all_gather | solution.py:77
  274.4 148.7 %while.16 = (s32[]{:T(128)}, f32[8,64,2048]{2,1,0:T(8,128)}, f32[8,64,16]{1,2,0:T(8,128)S(1)}, f32[8,64,16]{1,2,0:T(8,128)S(1)}, bf16[8,64,2048]{2,1,0:T(8,128)(...) while((s32[]{:T(128)}, f32[8,64,2048]{2,1,0:T(8,128)}, ...), condition=%wide.wide.region_5.6_spmd.clone, body=%wide.wide.region_0.5_spmd.clone.sunk | while | flops 1101201920 | bytes 71670264 | solution.py:49
  277.8 5.9 bitcast_reduce_fusion.6
  283.9 4.9 fusion.60
  296.4 5.9 bitcast_reduce_fusion.6
  315.0 5.9 bitcast_reduce_fusion.6
  321.2 4.9 fusion.60
  333.6 5.9 bitcast_reduce_fusion.6
  339.7 4.9 fusion.60
  352.2 5.9 bitcast_reduce_fusion.6
  358.3 4.9 fusion.60
  370.8 5.9 bitcast_reduce_fusion.6
  376.9 4.9 fusion.60
  389.4 5.9 bitcast_reduce_fusion.6
  395.5 4.9 fusion.60
  407.9 5.9 bitcast_reduce_fusion.6
  425.8 7.1 %all-to-all-start.4 = ((f32[64,1,128]{2,1,0:T(1,128)}), f32[64,1,128]{2,1,0:T(1,128)S(1)}, u32[]{:S(2)}, u32[]{:S(2)}) async-start(f32[64,1,128]{2,1,0:T(1,128)} %reshape.160), calls=%async_computation.4 | async-start | bytes 65536 | tf_op jit(solution)/shard_map/all_to_all | solution.py:82
  435.0 7.0 %all-to-all-done.4 = f32[64,1,128]{2,1,0:T(1,128)S(1)} async-done(((f32[64,1,128]{2,1,0:T(1,128)}), f32[64,1,128]{2,1,0:T(1,128)S(1)}, u32[]{:S(2)}, u32[]{:S(2)}) %all-to-all-start.4) | async-done | bytes 32800 | tf_op jit(solution)/shard_map/all_to_all | solution.py:82
  446.6 7.7 %broadcast_in_dim_reshape.10 = f32[1,512,2048]{2,0,1:T(1,128)} reshape(f32[8,64,2048]{2,1,0:T(8,128)} %get-tuple-element.69) | data formatting | bytes 8388608 | tf_op jit(solution)/shard_map/broadcast_in_dim;reshape | solution.py:80
  455.9 9.4 %all-to-all-start.2 = ((f32[1,512,2048]{2,0,1:T(1,128)}), f32[1,512,2048]{2,0,1:T(1,128)}, u32[]{:S(2)}, u32[]{:S(2)}) async-start(f32[1,512,2048]{2,0,1:T(1,128)} %broadcast_in_dim_reshape.10), calls=%async_computation.2 | async-start | bytes 8388608 | tf_op jit(solution)/shard_map/all_to_all | solution.py:80
  467.9 48.9 %all-to-all-done.2 = f32[1,512,2048]{2,0,1:T(1,128)} async-done(((f32[1,512,2048]{2,0,1:T(1,128)}), f32[1,512,2048]{2,0,1:T(1,128)}, u32[]{:S(2)}, u32[]{:S(2)}) %all-to-all-start.2) | async-done | bytes 4194336 | tf_op jit(solution)/shard_map/all_to_all | solution.py:80
  517.9 11.3 %multiply_reduce_fusion = f32[8,2048]{1,0:T(8,128)S(1)} fusion(f32[1,64,8,2048]{3,0,2,1:T(1,128)} %bitcast.10, f32[1,64,8,2048]{3,0,2,1:T(1,128)S(1)} %bitcast.129), kind=kLoop, calls=%fused_computation.35 | loop fusion | flops 2080768 | bytes 8454144 | tf_op jit(solution)/shard_map/reduce_sum | solution.py:86
  529.3 58.6 %all_to_all.88 = bf16[4,2,2048]{2,1,0:T(2,128)(2,1)S(1)} all-to-all(bf16[4,2,2048]{2,1,0:T(2,128)(2,1)S(1)} %divide_convert_fusion), channel_id=1, replica_groups=mesh['head'=4,'ctx'=64] {'head'}, dimensions={0} | all-to-all | bytes 65536 | tf_op jit(solution)/shard_map/all_to_all | solution.py:89
  (249 shorter events, 96.1 us)
Async XLA Ops:
  6.5 267.8 %all-gather.2.cloned.1.call-start = ((), (), s32[]{:S(2)}) async-start(), calls=%async_computation.6 | async-start | bytes 2129920 | tf_op jit(solution)/shard_map/all_gather | solution.py:77
  18.3 8.6 %all-to-all-start.1 = ((bf16[2,4,512]{2,0,1:T(2,128)(2,1)}), bf16[2,4,512]{2,0,1:T(2,128)(2,1)S(1)}, u32[]{:S(2)}, u32[]{:S(2)}) async-start(bf16[2,4,512]{2,0,1:T(2,128)(2,1)} %bitcast.143), calls=%async_computation.1 | async-start | bytes 16384 | tf_op jit(solution)/shard_map/all_to_all | solution.py:65
  23.2 251.2 %copy-start.1 = (s32[4,1,2]{2,1,0:T(1,128)}, s32[4,1,2]{2,1,0:T(1,128)S(1)}, u32[]{:S(2)}) copy-start(s32[4,1,2]{2,1,0:T(1,128)S(1)} %constant_dynamic-slice_fusion.1) | copy-start | bytes 100
  277.8 11.0 %copy-start.2 = (bf16[2,2048,128]{2,1,0:T(8,128)(2,1)S(1)}, bf16[2,2048,128]{2,1,0:T(8,128)(2,1)}, u32[]{:S(2)}) copy-start(bf16[2,2048,128]{2,1,0:T(8,128)(2,1)} %get-tuple-element.425) | copy-start | bytes 3145732 | tf_op jit(solution)/shard_map/while
  283.9 5.8 copy-start
  296.4 11.0 %copy-start.2 = (bf16[2,2048,128]{2,1,0:T(8,128)(2,1)S(1)}, bf16[2,2048,128]{2,1,0:T(8,128)(2,1)}, u32[]{:S(2)}) copy-start(bf16[2,2048,128]{2,1,0:T(8,128)(2,1)} %get-tuple-element.425) | copy-start | bytes 3145732 | tf_op jit(solution)/shard_map/while
  302.5 5.8 copy-start
  315.0 11.0 %copy-start.2 = (bf16[2,2048,128]{2,1,0:T(8,128)(2,1)S(1)}, bf16[2,2048,128]{2,1,0:T(8,128)(2,1)}, u32[]{:S(2)}) copy-start(bf16[2,2048,128]{2,1,0:T(8,128)(2,1)} %get-tuple-element.425) | copy-start | bytes 3145732 | tf_op jit(solution)/shard_map/while
  321.2 5.8 copy-start
  333.6 11.0 %copy-start.2 = (bf16[2,2048,128]{2,1,0:T(8,128)(2,1)S(1)}, bf16[2,2048,128]{2,1,0:T(8,128)(2,1)}, u32[]{:S(2)}) copy-start(bf16[2,2048,128]{2,1,0:T(8,128)(2,1)} %get-tuple-element.425) | copy-start | bytes 3145732 | tf_op jit(solution)/shard_map/while
  339.7 5.8 copy-start
  352.2 11.0 %copy-start.2 = (bf16[2,2048,128]{2,1,0:T(8,128)(2,1)S(1)}, bf16[2,2048,128]{2,1,0:T(8,128)(2,1)}, u32[]{:S(2)}) copy-start(bf16[2,2048,128]{2,1,0:T(8,128)(2,1)} %get-tuple-element.425) | copy-start | bytes 3145732 | tf_op jit(solution)/shard_map/while
  358.3 5.8 copy-start
  370.8 11.0 %copy-start.2 = (bf16[2,2048,128]{2,1,0:T(8,128)(2,1)S(1)}, bf16[2,2048,128]{2,1,0:T(8,128)(2,1)}, u32[]{:S(2)}) copy-start(bf16[2,2048,128]{2,1,0:T(8,128)(2,1)} %get-tuple-element.425) | copy-start | bytes 3145732 | tf_op jit(solution)/shard_map/while
  376.9 5.8 copy-start
  389.4 11.0 %copy-start.2 = (bf16[2,2048,128]{2,1,0:T(8,128)(2,1)S(1)}, bf16[2,2048,128]{2,1,0:T(8,128)(2,1)}, u32[]{:S(2)}) copy-start(bf16[2,2048,128]{2,1,0:T(8,128)(2,1)} %get-tuple-element.425) | copy-start | bytes 3145732 | tf_op jit(solution)/shard_map/while
  395.5 5.8 copy-start
  407.9 11.0 %copy-start.2 = (bf16[2,2048,128]{2,1,0:T(8,128)(2,1)S(1)}, bf16[2,2048,128]{2,1,0:T(8,128)(2,1)}, u32[]{:S(2)}) copy-start(bf16[2,2048,128]{2,1,0:T(8,128)(2,1)} %get-tuple-element.425) | copy-start | bytes 3145732 | tf_op jit(solution)/shard_map/while
  414.1 5.8 copy-start
  425.8 16.2 %all-to-all-start.4 = ((f32[64,1,128]{2,1,0:T(1,128)}), f32[64,1,128]{2,1,0:T(1,128)S(1)}, u32[]{:S(2)}, u32[]{:S(2)}) async-start(f32[64,1,128]{2,1,0:T(1,128)} %reshape.160), calls=%async_computation.4 | async-start | bytes 65536 | tf_op jit(solution)/shard_map/all_to_all | solution.py:82
  442.1 13.8 %all-to-all-start.3 = ((f32[64,1,128]{2,1,0:T(1,128)}), f32[64,1,128]{2,1,0:T(1,128)S(1)}, u32[]{:S(2)}, u32[]{:S(2)}) async-start(f32[64,1,128]{2,1,0:T(1,128)} %reshape.158), calls=%async_computation.3 | async-start | bytes 65536 | tf_op jit(solution)/shard_map/all_to_all | solution.py:81
  455.9 60.9 %all-to-all-start.2 = ((f32[1,512,2048]{2,0,1:T(1,128)}), f32[1,512,2048]{2,0,1:T(1,128)}, u32[]{:S(2)}, u32[]{:S(2)}) async-start(f32[1,512,2048]{2,0,1:T(1,128)} %broadcast_in_dim_reshape.10), calls=%async_computation.2 | async-start | bytes 8388608 | tf_op jit(solution)/shard_map/all_to_all | solution.py:80
Sparse Core Ops, SparseCore 0:
  18.5 255.8 all-gather.1
where the time goes:
time: 597 us; the launch traced here: 595 us
  waiting for transfers between devices  308 us (52%)
  matrix products  72.6 us (12%)
  blocking collectives  69.8 us (12%)
  other arithmetic  60.8 us (10%)
  local copies, waits for them, and re-layouts  44.5 us (7%)
  starting transfers between devices  25 us (4%)
  between operations  13.6 us (2%)
    all_gather x1, waiting for transfers between devices, shards(): q_all = lax.all_gather(q_own, 'ctx', axis=0, tiled=True)  247 us
    all_to_all x1, blocking collectives, shards(): lax.all_to_all(result, 'head', split_axis=0, concat_axis=1, tiled=True)  58.6 us
    all_to_all x1, waiting for transfers between devices, shards(): lax.all_to_all(part_out[None], 'ctx', split_axis=1, concat_axis=0, tiled=...  48.9 us
    dot_general x8, matrix products, attend(): jnp.einsum('rkgd,ksd->rkgs', q_four, keys_cached, preferred_element_type=...  47.2 us
    reduce_sum x16, other arithmetic, attend(): total = jnp.sum(p_cached, -1) + jnp.sum(p_fresh, -1)  39.2 us
    while x56, local copies, waits for them, and re-layouts  16.7 us
    dot_general x8, matrix products, attend(): jnp.einsum('rkgs,ksd->rkgd', p_cached.astype(jnp.bfloat16), values_cached...  13.8 us
  transfers between devices with their start and end apart: 5, of which 5 were waited for; matrix products, arithmetic and copies ran while one was open for 2% of the time, Pallas kernels for 0%

commit v1 on v0

v1 whole, which is shorter than its diff:
```python
import functools

import jax
import jax.numpy as jnp
from jax import lax
from jax.experimental import pallas as pl
from jax.experimental.pallas import tpu as pltpu
from jax.sharding import PartitionSpec as P

MESH = pl.DeviceIdType.MESH
masked = -1e30
NH = 4
NY = 2
COL = NH * NY
CHUNK = 256


def kernel(
    nx, nz, scale2,
    msg, ordq, lens, k_hbm, v_hbm,
    out,
    col, qall, kb, vb, vt, kf, vf, fresh_f, bias, plen, s_a, s_b, acc, part, xin, zpart, zin, fin, fout,
    col_s, col_r, len_s, len_r, kv_s, kv_r, own_sem, qz_s, qz_r, qx_s, qx_r,
    px_s, px_r, pz_s, pz_r, f_s, f_r,
):
    h = lax.axis_index("head")
    c = lax.axis_index("ctx")
    z = lax.rem(c, nz)
    y = lax.rem(lax.div(c, nz), NY)
    x = lax.div(c, nz * NY)
    u = y * NH + h
    slots = k_hbm.shape[1]
    rows = 128 * nx
    chunks = slots // CHUNK

    def at(h_, x_, y_, z_):
        return (h_, (x_ * NY + y_) * nz + z_)

    def col_peer(off):
        w = lax.rem(u + off, COL)
        return w, lax.rem(w, NH), lax.div(w, NH)

    def remote(src, dst, ss, rs, dev):
        return pltpu.make_async_remote_copy(
            src_ref=src, dst_ref=dst, send_sem=ss, recv_sem=rs, device_id=dev, device_id_type=MESH
        )

    def far(t):
        half = lax.div(t, 2)
        return jnp.where(lax.rem(t, 2) == 0, nz // 2 + half, nz // 2 - 1 - half)

    def plane(t):
        return lax.rem(z + far(t), nz)

    own = [
        pltpu.make_async_copy(k_hbm.at[y], kb.at[0], own_sem.at[0]),
        pltpu.make_async_copy(v_hbm.at[y], vb.at[0], own_sem.at[1]),
    ]
    for copy in own:
        copy.start()

    barrier = pltpu.get_barrier_semaphore()
    for off in range(1, COL):
        _, h_, y_ = col_peer(off)
        pl.semaphore_signal(barrier, inc=1, device_id=at(h_, x, y_, z), device_id_type=MESH)
    for off in range(1, nz):
        pl.semaphore_signal(
            barrier, inc=1, device_id=at(h, x, y, lax.rem(z + off, nz)), device_id_type=MESH
        )
    for off in range(1, nx):
        pl.semaphore_signal(
            barrier, inc=1, device_id=at(h, lax.rem(x + off, nx), y, z), device_id_type=MESH
        )
    pl.semaphore_wait(barrier, COL + nz + nx - 3)

    def col_copy(off):
        w, h_, y_ = col_peer(off)
        return remote(
            msg.at[NY * h_ + y_], col.at[u], col_s.at[w], col_r.at[u], at(h_, x, y_, z)
        )

    def col_arrival(off):
        w, h_, y_ = col_peer(off)
        return remote(msg.at[0], col.at[w], col_s.at[w], col_r.at[w], at(h_, x, y_, z))

    for off in range(1, COL):
        col_copy(off).start()
    partner = at(h, x, 1 - y, z)
    len_copy = remote(lens, plen, len_s, len_r, partner)
    len_copy.start()
    col[u] = msg[NY * h + y]
    for off in range(1, COL):
        col_arrival(off).wait_recv()

    base = pl.multiple_of(x * 128, 128)
    for w in range(COL):
        qall[z, pl.ds(pl.multiple_of(x * 128 + w * 16, 16), 16), :] = col[w, 0:16, :]

    def qz_copy(t):
        to = lax.rem(z + nz - far(t), nz)
        ref = qall.at[z, pl.ds(base, 128), :]
        return remote(ref, ref, qz_s.at[t], qz_r.at[t], at(h, x, y, to))

    def qz_arrival(t):
        ref = qall.at[plane(t), pl.ds(base, 128), :]
        return remote(ref, ref, qz_s.at[t], qz_r.at[t], at(h, x, y, plane(t)))

    def qx_copy(t, off):
        ref = qall.at[plane(t), pl.ds(base, 128), :]
        return remote(
            ref, ref, qx_s.at[t, off], qx_r.at[t, off], at(h, lax.rem(x + off, nx), y, z)
        )

    def qx_arrival(t, off):
        who = lax.rem(x + nx - off, nx)
        ref = qall.at[plane(t), pl.ds(pl.multiple_of(who * 128, 128), 128), :]
        return remote(ref, ref, qx_s.at[t, off], qx_r.at[t, off], at(h, who, y, z))

    for t in range(nz - 1):
        qz_copy(t).start()
    kv = [
        remote(k_hbm.at[1 - y], kb.at[1], kv_s.at[0], kv_r.at[0], partner),
        remote(v_hbm.at[1 - y], vb.at[1], kv_s.at[1], kv_r.at[1], partner),
    ]
    for copy in kv:
        copy.start()

    for span in range(2):
        side = y if span == 0 else 1 - y
        fresh_f[...] = jnp.zeros_like(fresh_f)
        for w in range(NH):
            block = col[side * NH + w, 16:32, :].astype(jnp.float32)
            fresh_f[0, 2 * w : 2 * w + 2, :] = block[0:2, :]
            fresh_f[1, 2 * w : 2 * w + 2, :] = block[2:4, :]
        kf[span] = fresh_f[0].astype(jnp.bfloat16)
        vf[span] = fresh_f[1].astype(jnp.bfloat16)

    def set_bias(span, length):
        for j in range(chunks):
            slot = lax.broadcasted_iota(jnp.int32, (CHUNK, 128), 0).astype(jnp.float32) + j * CHUNK
            bias[span, j * CHUNK : (j + 1) * CHUNK, :] = jnp.where(slot < length, 0.0, masked)

    def turn(span):
        for j in range(slots // 128):
            vt[span, :, j * 128 : (j + 1) * 128] = vb[span, j * 128 : (j + 1) * 128, :].T

    set_bias(0, lens[0:1, :])
    for copy in own:
        copy.wait()
    turn(0)

    tile_row = lax.broadcasted_iota(jnp.int32, (8, 128), 0)
    for d in range(nz):
        for w in range(nx):
            part[d, w, 0:128, :] = jnp.zeros((128, 128), jnp.float32)
            part[d, w, 128:136, :] = jnp.where(tile_row == 0, masked, 0.0)

    mine = ordq[z, :, pl.ds(base, 128)]
    lane = lax.broadcasted_iota(jnp.int32, (8, 128), 1)

    def key_order(side):
        hit = lax.div(lane, 8) == tile_row + 8 * side
        return jnp.max(jnp.where(hit, mine, -1.0), axis=1, keepdims=True)

    fresh_order = (key_order(y), key_order(1 - y))

    for t in range(nz - 1):
        qz_arrival(t).wait_recv()
        for off in range(1, nx):
            qx_copy(t, off).start()
    for off in range(1, nx):
        qx_copy(nz - 1, off).start()

    def scores(span, d, s_ref, j, m):
        keys = kb[span, j * CHUNK : (j + 1) * CHUNK, :]
        s = lax.dot_general(
            keys, qall[d], (((1,), (1,)), ((), ())), preferred_element_type=jnp.float32
        )
        s = s + jnp.concatenate([bias[span, j * CHUNK : (j + 1) * CHUNK, :]] * nx, axis=1)
        s_ref[j * CHUNK : (j + 1) * CHUNK, :] = s
        top = jnp.max(s.reshape(CHUNK // 8, 8, rows), axis=0)
        return top if m is None else jnp.maximum(m, top)

    def fresh_scores(span, d, s_ref, m):
        s = lax.dot_general(
            kf[span], qall[d], (((1,), (1,)), ((), ())), preferred_element_type=jnp.float32
        )
        key = jnp.where(span == 0, fresh_order[0], fresh_order[1])
        s = jnp.where(key <= ordq[d], s[0:8, :], masked)
        s_ref[slots : slots + 8, :] = s
        return jnp.maximum(m, s)

    def weights(span, s_ref, j, peak, total):
        p = jnp.exp2(s_ref[j * CHUNK : (j + 1) * CHUNK, :] * scale2 - peak)
        total = total + jnp.sum(p.reshape(CHUNK // 8, 8, rows), axis=0)
        values = vt[span, :, j * CHUNK : (j + 1) * CHUNK]
        more = jnp.dot(values, p.astype(jnp.bfloat16), preferred_element_type=jnp.float32)
        if j == 0:
            acc[...] = more
        else:
            acc[...] += more
        return total

    def fresh_weights(span, s_ref, peak, total):
        p = jnp.exp2(s_ref[slots : slots + 8, :] * scale2 - peak)
        both = jnp.concatenate([p, jnp.zeros_like(p)], axis=0).astype(jnp.bfloat16)
        acc[...] += lax.dot_general(
            vf[span], both, (((0,), (0,)), ((), ())), preferred_element_type=jnp.float32
        )
        return total + p

    def add_part(d, peak, total):
        total = jnp.sum(total, axis=0, keepdims=True)
        for w in range(nx):
            cut = slice(w * 128, (w + 1) * 128)
            old = part[d, w, 128:136, :]
            new_peak = jnp.maximum(old[0:1, :], peak[:, cut])
            keep = jnp.exp2(old[0:1, :] - new_peak)
            take = jnp.exp2(peak[:, cut] - new_peak)
            part[d, w, 0:128, :] = part[d, w, 0:128, :] * keep + acc[:, cut] * take
            new_total = old[1:2, :] * keep + total[:, cut] * take
            part[d, w, 128:136, :] = jnp.where(tile_row == 0, new_peak, new_total)

    def step(t, s_now, s_next, m, ahead):
        span = lax.div(t, nz)
        d = plane(lax.rem(t, nz))
        span_n = lax.div(t + 1, nz)
        d_n = plane(lax.rem(t + 1, nz))
        peak = jnp.max(m, axis=0, keepdims=True) * scale2
        total = jnp.zeros((8, rows), jnp.float32)
        nxt = None
        for j in range(chunks):
            if ahead:
                nxt = scores(span_n, d_n, s_next, j, nxt)
            total = weights(span, s_now, j, peak, total)
        if ahead:
            nxt = fresh_scores(span_n, d_n, s_next, nxt)
        total = fresh_weights(span, s_now, peak, total)
        add_part(d, peak, total)
        return nxt

    def px_copy(t, off):
        who = lax.rem(x + off, nx)
        d = plane(t)
        return remote(part.at[d, who], xin.at[d, x], px_s.at[t, off], px_r.at[t, off], at(h, who, y, z))

    def px_arrival(t, off):
        who = lax.rem(x + nx - off, nx)
        d = plane(t)
        return remote(part.at[d, who], xin.at[d, who], px_s.at[t, off], px_r.at[t, off], at(h, who, y, z))

    def pz_copy(t):
        d = plane(t)
        return remote(zpart.at[d], zin.at[t], pz_s.at[t], pz_r.at[t], at(h, x, y, d))

    def pz_arrival(t):
        who = lax.rem(z + nz - far(t), nz)
        return remote(zpart.at[who], zin.at[t], pz_s.at[t], pz_r.at[t], at(h, x, y, who))

    def merged(tiles, blocks):
        peak = functools.reduce(jnp.maximum, [tile[0:1, :] for tile in tiles])
        factors = [jnp.exp2(tile[0:1, :] - peak) for tile in tiles]
        total = sum(tile[1:2, :] * f for tile, f in zip(tiles, factors))
        value = sum(block * f for block, f in zip(blocks, factors))
        return peak, total, value

    def merge_x(t):
        d = plane(t)
        for off in range(1, nx):
            px_arrival(t, off).wait_recv()
        tiles, blocks = [part[d, x, 128:136, :]], [part[d, x, 0:128, :]]
        for off in range(1, nx):
            who = lax.rem(x + off, nx)
            tiles.append(xin[d, who, 128:136, :])
            blocks.append(xin[d, who, 0:128, :])
        peak, total, value = merged(tiles, blocks)
        zpart[d, 0:128, :] = value
        zpart[d, 128:136, :] = jnp.where(tile_row == 0, peak, total)

    def need_q(t):
        for off in range(1, nx):
            qx_arrival(t, off).wait_recv()

    def before(t):
        @pl.when(t + 1 < nz)
        def _():
            need_q(t + 1)

        @pl.when(t + 1 == nz)
        def _():
            len_copy.wait_recv()
            kv[0].wait_recv()
            set_bias(1, plen[0:1, :])

        @pl.when(t == nz)
        def _():
            kv[1].wait_recv()
            turn(1)

    def after(t):
        @pl.when(t >= nz)
        def _():
            for off in range(1, nx):
                px_copy(t - nz, off).start()

        @pl.when(t >= nz + 1)
        def _():
            merge_x(t - nz - 1)
            pz_copy(t - nz - 1).start()

    need_q(0)
    m = None
    for j in range(chunks):
        m = scores(0, plane(0), s_a, j, m)
    m = fresh_scores(0, plane(0), s_a, m)

    def pair(i, m):
        t = 2 * i
        before(t)
        m = step(t, s_a, s_b, m, True)
        after(t)
        before(t + 1)
        m = step(t + 1, s_b, s_a, m, True)
        after(t + 1)
        return m

    m = lax.fori_loop(0, nz - 1, pair, m)
    last = 2 * nz - 2
    before(last)
    m = step(last, s_a, s_b, m, True)
    after(last)
    step(last + 1, s_b, s_a, m, False)
    after(last + 1)

    merge_x(nz - 1)
    tiles, blocks = [zpart[z, 128:136, :]], [zpart[z, 0:128, :]]
    for t in range(nz - 1):
        pz_arrival(t).wait_recv()
        tiles.append(zin[t, 128:136, :])
        blocks.append(zin[t, 0:128, :])
    peak, total, value = merged(tiles, blocks)
    fout[...] = (value / total).T.astype(jnp.bfloat16)

    def home(off):
        w, h_, y_ = col_peer(off)
        src = fout.at[pl.ds(pl.multiple_of(w * 16, 16), 16), :]
        return remote(src, fin.at[NY * h + y], f_s.at[w], f_r.at[u], at(h_, x, y_, z))

    def home_arrival(off):
        w, h_, y_ = col_peer(off)
        src = fout.at[pl.ds(0, 16), :]
        return remote(src, fin.at[NY * h_ + y_], f_s.at[w], f_r.at[w], at(h_, x, y_, z))

    for off in range(1, COL):
        home(off).start()
    fin[NY * h + y] = fout[pl.ds(pl.multiple_of(u * 16, 16), 16), :]
    for off in range(1, COL):
        home_arrival(off).wait_recv()
    out[...] = fin[...]

    for off in range(1, COL):
        col_copy(off).wait_send()
        home(off).wait_send()
    len_copy.wait_send()
    for copy in kv:
        copy.wait_send()
    for t in range(nz):
        for off in range(1, nx):
            qx_copy(t, off).wait_send()
            px_copy(t, off).wait_send()
        if t < nz - 1:
            qz_copy(t).wait_send()
            pz_copy(t).wait_send()


def shards(nx, nz, q_new, kv_new, k_cache, v_cache, span_len, order):
    kv_dev, slots, width = k_cache.shape
    tokens = q_new.shape[0]
    kv_heads = NH * kv_dev
    group = q_new.shape[1] // (kv_heads * width)
    rows = 128 * nx
    bf = jnp.bfloat16
    queries = q_new.reshape(tokens, kv_heads, group, width).transpose(1, 0, 2, 3)
    queries = queries.reshape(kv_heads, tokens * group, width)
    fresh = kv_new.reshape(tokens, kv_heads, 2, width).transpose(1, 2, 0, 3)
    fresh = fresh.reshape(kv_heads, 2 * tokens, width)
    pad = jnp.zeros((kv_heads, 16 - 2 * tokens, width), bf)
    msg = jnp.concatenate([queries, fresh, pad], axis=1)
    grid = order.astype(jnp.float32).reshape(NH, nx, NY, nz, tokens).transpose(3, 1, 2, 0, 4)
    grid = jnp.broadcast_to(grid.reshape(nz, 1, rows // group, 1), (nz, 8, rows // group, group))
    ordq = grid.reshape(nz, 8, rows)
    lens = jnp.broadcast_to(span_len.astype(jnp.float32).reshape(1, 1), (8, 128))
    scale2 = width ** (-0.5) * 1.4426950408889634
    vmem = pl.BlockSpec(memory_space=pltpu.VMEM)
    hbm = pl.BlockSpec(memory_space=pltpu.HBM)
    f32 = jnp.float32
    dma = pltpu.SemaphoreType.DMA
    out = pl.pallas_call(
        functools.partial(kernel, nx, nz, scale2),
        out_shape=jax.ShapeDtypeStruct((kv_heads, tokens * group, width), bf),
        in_specs=[vmem, vmem, vmem, hbm, hbm],
        out_specs=vmem,
        scratch_shapes=[
            pltpu.VMEM((COL, 32, width), bf),
            pltpu.VMEM((nz, rows, width), bf),
            pltpu.VMEM((2, slots, width), bf),
            pltpu.VMEM((2, slots, width), bf),
            pltpu.VMEM((2, width, slots), bf),
            pltpu.VMEM((2, 16, width), bf),
            pltpu.VMEM((2, 16, width), bf),
            pltpu.VMEM((2, 16, width), f32),
            pltpu.VMEM((2, slots, 128), f32),
            pltpu.VMEM((8, 128), f32),
            pltpu.VMEM((slots + 8, rows), f32),
            pltpu.VMEM((slots + 8, rows), f32),
            pltpu.VMEM((width, rows), f32),
            pltpu.VMEM((nz, nx, width + 8, 128), f32),
            pltpu.VMEM((nz, nx, width + 8, 128), f32),
            pltpu.VMEM((nz, width + 8, 128), f32),
            pltpu.VMEM((nz, width + 8, 128), f32),
            pltpu.VMEM((kv_heads, 16, width), bf),
            pltpu.VMEM((128, width), bf),
            dma((COL,)), dma((COL,)), dma, dma, dma((2,)), dma((2,)), dma((2,)),
            dma((nz,)), dma((nz,)), dma((nz, nx)), dma((nz, nx)),
            dma((nz, nx)), dma((nz, nx)), dma((nz,)), dma((nz,)), dma((COL,)), dma((COL,)),
        ],
        compiler_params=pltpu.CompilerParams(
            collective_id=0, has_side_effects=True, vmem_limit_bytes=48 << 20
        ),
    )(msg, ordq, lens, k_cache, v_cache)
    out = out.reshape(kv_heads, tokens, group, width).transpose(1, 0, 2, 3)
    return out.reshape(tokens, kv_heads * group * width)


def solution(mesh):
    nz = 8
    nx = mesh.shape["ctx"] // (nz * NY)
    return jax.shard_map(
        functools.partial(shards, nx, nz),
        mesh=mesh,
        in_specs=(
            P(("head", "ctx"), None),
            P(("head", "ctx"), None),
            P("head", "ctx", None),
            P("head", "ctx", None),
            P("ctx"),
            P(),
        ),
        out_specs=P(("head", "ctx"), None),
        check_vma=False,
    )
```

time: 597 us -> 81.3 us (0.14)
  waiting for transfers between devices: 308 us -> 0 us
  Pallas kernels: 0 us -> 76 us
  matrix products: 72.6 us -> 0 us
  blocking collectives: 69.8 us -> 0 us
  other arithmetic: 60.8 us -> 0.85 us
  local copies, waits for them, and re-layouts: 44.5 us -> 3.51 us
  starting transfers between devices: 25 us -> 0 us
  between operations: 13.6 us -> 0.73 us
    all_gather x1 -> x0, waiting for transfers between devices: 247 us -> none  [shards(): q_all = lax.all_gather(q_own, 'ctx', axis=0, tiled=True)]
    pallas_call x0 -> x1, Pallas kernels: none -> 76 us  [shards(): pl.pallas_call(functools.partial(kernel, nx, nz, scale2), out_shape=jax.S...]
    dot_general x32 -> x0, matrix products: 72.6 us -> none  [the longest x8 47.2 us: attend(): jnp.einsum('rkgd,ksd->rkgs', q_four, keys_cached, preferred_element_type=...]
    all_to_all x2 -> x0, blocking collectives: 69.8 us -> none  [the longest x1 58.6 us: shards(): lax.all_to_all(result, 'head', split_axis=0, concat_axis=1, tiled=True)]
    all_to_all x4 -> x0, waiting for transfers between devices: 60.9 us -> none  [the longest x1 48.9 us: shards(): lax.all_to_all(part_out[None], 'ctx', split_axis=1, concat_axis=0, tiled=...]
    reduce_sum x18 -> x0, other arithmetic: 50.6 us -> none  [the longest x16 39.2 us: attend(): total = jnp.sum(p_cached, -1) + jnp.sum(p_fresh, -1)]
    all_to_all x4 -> x0, starting transfers between devices: 25 us -> none  [the longest x1 9.37 us: shards(): lax.all_to_all(part_out[None], 'ctx', split_axis=1, concat_axis=0, tiled=...]
    while x56 -> x0, local copies, waits for them, and re-layouts: 16.7 us -> none
  transfers between devices with their start and end apart: 5 -> 0, of which waited for: 5 -> 0; matrix products, arithmetic and copies ran while one was open for 2% -> 0% of each run, Pallas kernels for 0% -> 0%
where the time goes in v1:
time: 81.3 us; the launch traced here: 81.1 us
  Pallas kernels  76 us (93%)
  local copies, waits for them, and re-layouts  3.51 us (4%)
  other arithmetic  0.85 us (1%)
    pallas_call x1, Pallas kernels, shards(): pl.pallas_call(functools.partial(kernel, nx, nz, scale2), out_shape=jax.S...  76 us
    unnamed x8, local copies, waits for them, and re-layouts  1.88 us

profile of v1, /device:TPU:1, one launch (start us, length us, event | category | flops | bytes accessed | tf_op | source)
XLA Modules:
  0.0 81.1 jit_solution(11665965682186469560)
XLA Ops:
  0.0 0.0 copy-start
  0.0 0.8 convert_element_type.6
  0.8 0.1 reshape.31
  0.9 0.3 copy.12
  1.2 0.1 copy.13
  1.2 0.1 broadcast_in_dim.23
  1.4 0.2 broadcast_in_dim.24
  1.6 0.0 copy-start.2
  1.6 0.8 copy_bitcast_fusion.3
  2.4 0.1 pad.2.clone
  2.4 0.0 copy-done.2
  2.4 0.1 maximum_maximum_fusion.msg
  3.2 0.0 copy-done
  3.2 0.0 copy-start.1
  3.2 1.2 %copy-done.1 = bf16[2,2048,128]{2,1,0:T(8,128)(2,1)S(1)} copy-done((bf16[2,2048,128]{2,1,0:T(8,128)(2,1)S(1)}, bf16[2,2048,128]{2,1,0:T(8,128)(2,1)}, u32[]{:S(2)}) %copy-start.1) | copy-done | bytes 1048600
  4.4 76.0 %shard_map.64 = bf16[8,16,128]{2,1,0:T(8,128)(2,1)S(1)} custom-call(bf16[8,32,128]{2,1,0:T(8,128)(2,1)S(1)} %maximum_maximum_fusion.msg, f32[8,8,512]{2,1,0:T(8,128)S(1)} %broadcast_in_dim.25.ordq, f32[8,128]{1,0:T(8,128)S(1)} %broadcast_in_dim.27.lens, bf16[2,2048,128]{2,1,0:T(8,128)(2,1)S(1)} %copy-done, bf16[2,2048,128]{2,1,0:T(8,128)(2,1)S(1)} %copy-done.1), custom_call_target="tpu_custom_call" | custom-call | tf_op jit(solution)/shard_map/pallas_call | solution.py:398
  80.5 0.6 copy.22
  (4 shorter events, 0.0 us)
Async XLA Ops:
  0.0 3.2 %copy-start = (bf16[2,2048,128]{2,1,0:T(8,128)(2,1)S(1)}, bf16[2,2048,128]{2,1,0:T(8,128)(2,1)}, u32[]{:S(2)}) copy-start(bf16[2,2048,128]{2,1,0:T(8,128)(2,1)} %k_hbm.1) | copy-start | bytes 3145732
  1.6 0.9 %copy-start.2 = (bf16[2,2048]{1,0:T(2,128)(2,1)S(1)}, bf16[2,2048]{1,0:T(2,128)(2,1)}, u32[]{:S(2)}) copy-start(bf16[2,2048]{1,0:T(2,128)(2,1)} %param.7) | copy-start | bytes 24580
  3.2 1.2 %copy-start.1 = (bf16[2,2048,128]{2,1,0:T(8,128)(2,1)S(1)}, bf16[2,2048,128]{2,1,0:T(8,128)(2,1)}, u32[]{:S(2)}) copy-start(bf16[2,2048,128]{2,1,0:T(8,128)(2,1)} %v_hbm.1) | copy-start | bytes 3145732

commit v2 on v1

v2 whole, which is shorter than its diff:
```python
import functools

import jax
import jax.numpy as jnp
from jax import lax
from jax.experimental import pallas as pl
from jax.experimental.pallas import tpu as pltpu
from jax.sharding import PartitionSpec as P

MESH = pl.DeviceIdType.MESH
masked = -1e30
NH = 4
NY = 2
COL = NH * NY
CHUNK = 256


def kernel(
    nx, nz, scale2,
    q_hbm, f_hbm, len_smem, ord_hbm, k_hbm, v_hbm,
    out,
    q_in, f_in, ord_in, msg, ordq, lens,
    col, qall, kb, vb, vt, kf, vf, fresh_f, bias, plen, s_a, s_b, acc, part,
    xout, xin, zout, zin, fin, fout,
    col_s, col_r, len_s, len_r, kv_s, kv_r, own_sem, qz_s, qz_r, qx_s, qx_r,
    px_s, px_r, pz_s, pz_r, f_s, f_r,
):
    h = lax.axis_index("head")
    c = lax.axis_index("ctx")
    z = lax.rem(c, nz)
    y = lax.rem(lax.div(c, nz), NY)
    x = lax.div(c, nz * NY)
    u = y * NH + h
    slots = k_hbm.shape[1]
    rows = 128 * nx
    chunks = slots // CHUNK

    def at(h_, x_, y_, z_):
        return (h_, (x_ * NY + y_) * nz + z_)

    def col_peer(off):
        w = lax.rem(u + off, COL)
        return w, lax.rem(w, NH), lax.div(w, NH)

    def remote(src, dst, ss, rs, dev):
        return pltpu.make_async_remote_copy(
            src_ref=src, dst_ref=dst, send_sem=ss, recv_sem=rs, device_id=dev, device_id_type=MESH
        )

    def far(t):
        half = lax.div(t, 2)
        return jnp.where(lax.rem(t, 2) == 0, nz // 2 + half, nz // 2 - 1 - half)

    def plane(t):
        return lax.rem(z + far(t), nz)

    own = [
        pltpu.make_async_copy(k_hbm.at[y], kb.at[0], own_sem.at[0]),
        pltpu.make_async_copy(v_hbm.at[y], vb.at[0], own_sem.at[1]),
    ]
    small = [
        pltpu.make_async_copy(q_hbm, q_in, own_sem.at[2]),
        pltpu.make_async_copy(f_hbm, f_in, own_sem.at[3]),
        pltpu.make_async_copy(ord_hbm, ord_in, own_sem.at[4]),
    ]
    for copy in small + own:
        copy.start()

    barrier = pltpu.get_barrier_semaphore()
    for off in range(1, COL):
        _, h_, y_ = col_peer(off)
        pl.semaphore_signal(barrier, inc=1, device_id=at(h_, x, y_, z), device_id_type=MESH)
    for off in range(1, nz):
        pl.semaphore_signal(
            barrier, inc=1, device_id=at(h, x, y, lax.rem(z + off, nz)), device_id_type=MESH
        )
    for off in range(1, nx):
        pl.semaphore_signal(
            barrier, inc=1, device_id=at(h, lax.rem(x + off, nx), y, z), device_id_type=MESH
        )

    tile_row = lax.broadcasted_iota(jnp.int32, (8, 128), 0)
    pair_row = lax.broadcasted_iota(jnp.int32, (16, 128), 0)
    lens[...] = jnp.zeros((8, 128), jnp.float32) + len_smem[0].astype(jnp.float32)

    def set_bias(span, length):
        for j in range(chunks):
            slot = lax.broadcasted_iota(jnp.int32, (CHUNK, 128), 0).astype(jnp.float32) + j * CHUNK
            bias[span, j * CHUNK : (j + 1) * CHUNK, :] = jnp.where(slot < length, 0.0, masked)

    set_bias(0, lens[0:1, :])
    for d in range(nz):
        for w in range(nx):
            part[d, w, 0:128, :] = jnp.zeros((128, 128), jnp.float32)
            part[d, w, 128:136, :] = jnp.where(tile_row == 0, masked, 0.0)
    for copy in small:
        copy.wait()
    for w in range(COL):
        msg[w, 0:16, :] = q_in[w * 16 : (w + 1) * 16, :]
        msg[w, 16:32, :] = f_in[w // 4 * 16 : w // 4 * 16 + 16, :]

    places = ord_in.shape[1]
    pos = ord_in[...]
    high, low = lax.div(pos, 16), lax.rem(pos, 16)
    digits = jnp.concatenate([high, low], axis=0).astype(jnp.float32).astype(jnp.bfloat16)
    lane = lax.broadcasted_iota(jnp.int32, (places, rows), 1)
    place = lax.broadcasted_iota(jnp.int32, (places, rows), 0)
    source = lax.div(lane, 64) * (2 * nz) + lax.rem(lane, 2)
    lane8 = lax.broadcasted_iota(jnp.int32, (8, rows), 1)
    picked = lax.rem(lax.div(lane8, 16), NH) == lax.rem(lax.broadcasted_iota(jnp.int32, (8, rows), 0), NH)
    for d in range(nz):
        pick = jnp.where(place == source + 2 * d, 1.0, 0.0).astype(jnp.bfloat16)
        both = jnp.dot(digits, pick, preferred_element_type=jnp.float32)
        both = jnp.where(picked, both, 0.0) * jnp.where(
            lax.broadcasted_iota(jnp.int32, (8, rows), 0) < NH, 16.0, 1.0
        )
        ordq[d] = jnp.broadcast_to(jnp.sum(both, axis=0, keepdims=True), (8, rows))

    pl.semaphore_wait(barrier, COL + nz + nx - 3)

    def col_copy(off):
        w, h_, y_ = col_peer(off)
        return remote(
            msg.at[NY * h_ + y_], col.at[u], col_s.at[w], col_r.at[u], at(h_, x, y_, z)
        )

    def col_arrival(off):
        w, h_, y_ = col_peer(off)
        return remote(msg.at[0], col.at[w], col_s.at[w], col_r.at[w], at(h_, x, y_, z))

    for off in range(1, COL):
        col_copy(off).start()
    partner = at(h, x, 1 - y, z)
    len_copy = remote(lens, plen, len_s, len_r, partner)
    len_copy.start()
    kv = [
        remote(k_hbm.at[1 - y], kb.at[1], kv_s.at[0], kv_r.at[0], partner),
        remote(v_hbm.at[1 - y], vb.at[1], kv_s.at[1], kv_r.at[1], partner),
    ]
    for copy in kv:
        copy.start()
    col[u] = msg[NY * h + y]

    def turn(span):
        for j in range(slots // 128):
            vt[span, :, j * 128 : (j + 1) * 128] = vb[span, j * 128 : (j + 1) * 128, :].T

    for copy in own:
        copy.wait()
    turn(0)
    for off in range(1, COL):
        col_arrival(off).wait_recv()

    base = pl.multiple_of(x * 128, 128)
    for w in range(COL):
        qall[z, pl.ds(pl.multiple_of(x * 128 + w * 16, 16), 16), :] = col[w, 0:16, :]

    def qz_copy(t):
        to = lax.rem(z + nz - far(t), nz)
        ref = qall.at[z, pl.ds(base, 128), :]
        return remote(ref, ref, qz_s.at[t], qz_r.at[t], at(h, x, y, to))

    def qz_arrival(t):
        ref = qall.at[plane(t), pl.ds(base, 128), :]
        return remote(ref, ref, qz_s.at[t], qz_r.at[t], at(h, x, y, plane(t)))

    def qx_copy(t, off):
        ref = qall.at[plane(t), pl.ds(base, 128), :]
        return remote(
            ref, ref, qx_s.at[t, off], qx_r.at[t, off], at(h, lax.rem(x + off, nx), y, z)
        )

    def qx_arrival(t, off):
        who = lax.rem(x + nx - off, nx)
        ref = qall.at[plane(t), pl.ds(pl.multiple_of(who * 128, 128), 128), :]
        return remote(ref, ref, qx_s.at[t, off], qx_r.at[t, off], at(h, who, y, z))

    for off in range(1, nx):
        qx_copy(nz - 1, off).start()
    for k in reversed(range(nz - 1)):
        qz_copy(k).start()

    for span in range(2):
        side = y if span == 0 else 1 - y
        fresh_f[1:3] = jnp.zeros((2, 16, 128), jnp.float32)
        first = 4 * lax.rem(NY * h + y, 4)
        for w in range(NH):
            fresh_f[0] = col[side * NH + w, 16:32, :].astype(jnp.float32)
            fresh_f[1, 2 * w : 2 * w + 2, :] = fresh_f[0, pl.ds(first, 2), :]
            fresh_f[2, 2 * w : 2 * w + 2, :] = fresh_f[0, pl.ds(first + 2, 2), :]
        kf[span] = fresh_f[1].astype(jnp.bfloat16)
        vf[span] = fresh_f[2].astype(jnp.bfloat16)

    mine = ordq[z, :, pl.ds(base, 128)]
    lane = lax.broadcasted_iota(jnp.int32, (8, 128), 1)

    def key_order(side):
        hit = lax.div(lane, 16) == lax.div(tile_row, 2) + NH * side
        hit = hit & (lax.rem(lane, 2) == lax.rem(tile_row, 2))
        return jnp.max(jnp.where(hit, mine, -1.0), axis=1, keepdims=True)

    fresh_order = (key_order(y), key_order(1 - y))

    def forward(k):
        qz_arrival(k).wait_recv()
        for off in range(1, nx):
            qx_copy(k, off).start()

    for t in range(1, min(3, nz)):
        forward(nz - 1 - t)

    def scores(span, d, s_ref, j, m):
        keys = kb[span, j * CHUNK : (j + 1) * CHUNK, :]
        s = lax.dot_general(
            keys, qall[d], (((1,), (1,)), ((), ())), preferred_element_type=jnp.float32
        )
        s = s + jnp.concatenate([bias[span, j * CHUNK : (j + 1) * CHUNK, :]] * nx, axis=1)
        s_ref[j * CHUNK : (j + 1) * CHUNK, :] = s
        top = jnp.max(s.reshape(CHUNK // 8, 8, rows), axis=0)
        return top if m is None else jnp.maximum(m, top)

    def fresh_scores(span, d, s_ref, m):
        s = lax.dot_general(
            kf[span], qall[d], (((1,), (1,)), ((), ())), preferred_element_type=jnp.float32
        )
        key = jnp.where(span == 0, fresh_order[0], fresh_order[1])
        s = jnp.where(key <= ordq[d], s[0:8, :], masked)
        s_ref[slots : slots + 8, :] = s
        return jnp.maximum(m, s)

    def weights(span, s_ref, j, peak, total):
        p = jnp.exp2(s_ref[j * CHUNK : (j + 1) * CHUNK, :] * scale2 - peak)
        total = total + jnp.sum(p.reshape(CHUNK // 8, 8, rows), axis=0)
        values = vt[span, :, j * CHUNK : (j + 1) * CHUNK]
        more = jnp.dot(values, p.astype(jnp.bfloat16), preferred_element_type=jnp.float32)
        if j == 0:
            acc[...] = more
        else:
            acc[...] += more
        return total

    def fresh_weights(span, s_ref, peak, total):
        p = jnp.exp2(s_ref[slots : slots + 8, :] * scale2 - peak)
        both = jnp.concatenate([p, jnp.zeros_like(p)], axis=0).astype(jnp.bfloat16)
        acc[...] += lax.dot_general(
            vf[span], both, (((0,), (0,)), ((), ())), preferred_element_type=jnp.float32
        )
        return total + p

    def add_part(d, peak, total):
        total = jnp.sum(total, axis=0, keepdims=True)
        for w in range(nx):
            cut = slice(w * 128, (w + 1) * 128)
            old = part[d, w, 128:136, :]
            new_peak = jnp.maximum(old[0:1, :], peak[:, cut])
            keep = jnp.exp2(old[0:1, :] - new_peak)
            take = jnp.exp2(peak[:, cut] - new_peak)
            part[d, w, 0:128, :] = part[d, w, 0:128, :] * keep + acc[:, cut] * take
            new_total = old[1:2, :] * keep + total[:, cut] * take
            part[d, w, 128:136, :] = jnp.where(tile_row == 0, new_peak, new_total)

    def order_of(t):
        return jnp.where(t < nz, nz - 1 - t, t - nz)

    def step(t, s_now, s_next, m, ahead):
        span, d = lax.div(t, nz), plane(order_of(t))
        span_n, d_n = lax.div(t + 1, nz), plane(order_of(t + 1))
        peak = jnp.max(m, axis=0, keepdims=True) * scale2
        total = jnp.zeros((8, rows), jnp.float32)
        nxt = None
        for j in range(chunks):
            if ahead:
                nxt = scores(span_n, d_n, s_next, j, nxt)
            total = weights(span, s_now, j, peak, total)
        if ahead:
            nxt = fresh_scores(span_n, d_n, s_next, nxt)
        total = fresh_weights(span, s_now, peak, total)
        add_part(d, peak, total)
        return nxt

    def encode(ref, value, peak, total, peak_total):
        size = jnp.maximum(jnp.max(jnp.abs(value), axis=0, keepdims=True), 1e-30)
        power = jnp.ceil(jnp.log2(size) + peak + 1e-3) - 15.0
        power_t = jnp.ceil(jnp.log2(total) + peak_total + 1e-3) - 15.0
        units = value * jnp.exp2(peak - power)
        units = (units + 12582912.0) - 12582912.0
        whole = total * jnp.exp2(peak_total - power_t)
        high = jnp.floor(whole)
        low = jnp.floor((whole - high) * 32767.0)
        tail = jnp.where(pair_row == 0, power, jnp.where(pair_row == 1, power_t, high))
        tail = jnp.where(pair_row == 3, low, tail)
        ref[0:128, :] = units.astype(jnp.int32).astype(jnp.int16)
        ref[128:144, :] = tail.astype(jnp.int32).astype(jnp.int16)

    def decode(ref):
        tail = ref[128:144, :].astype(jnp.int32).astype(jnp.float32)
        total = tail[2:3, :] + tail[3:4, :] * (1.0 / 32767.0)
        return ref[0:128, :].astype(jnp.int32).astype(jnp.float32), tail[0:1, :], total, tail[1:2, :]

    def merged(items):
        peak = functools.reduce(jnp.maximum, [item[1] for item in items])
        peak_total = functools.reduce(jnp.maximum, [item[3] for item in items])
        value = sum(item[0] * jnp.exp2(item[1] - peak) for item in items)
        total = sum(item[2] * jnp.exp2(item[3] - peak_total) for item in items)
        return value, peak, total, peak_total

    def px_copy(k, off):
        who = lax.rem(x + off, nx)
        return remote(xout.at[k, off], xin.at[k, off], px_s.at[k, off], px_r.at[k, off], at(h, who, y, z))

    def px_arrival(k, off):
        who = lax.rem(x + nx - off, nx)
        return remote(xout.at[k, off], xin.at[k, off], px_s.at[k, off], px_r.at[k, off], at(h, who, y, z))

    def pz_copy(k):
        return remote(zout.at[k], zin.at[k], pz_s.at[k], pz_r.at[k], at(h, x, y, plane(k)))

    def pz_arrival(k):
        who = lax.rem(z + nz - far(k), nz)
        return remote(zout.at[k], zin.at[k], pz_s.at[k], pz_r.at[k], at(h, x, y, who))

    def send_x(k):
        d = plane(k)
        for off in range(1, nx):
            who = lax.rem(x + off, nx)
            tile = part[d, who, 128:136, :]
            encode(xout.at[k, off], part[d, who, 0:128, :], tile[0:1, :], tile[1:2, :], tile[0:1, :])
            px_copy(k, off).start()

    def merge_x(k):
        tile = part[plane(k), x, 128:136, :]
        items = [(part[plane(k), x, 0:128, :], tile[0:1, :], tile[1:2, :], tile[0:1, :])]
        for off in range(1, nx):
            px_arrival(k, off).wait_recv()
            items.append(decode(xin.at[k, off]))
        return merged(items)

    def send_z(k):
        encode(zout.at[k], *merge_x(k))
        pz_copy(k).start()

    def need_q(t):
        for off in range(1, nx):
            qx_arrival(nz - 1 - t, off).wait_recv()

    def before(t):
        @pl.when(t + 3 < nz)
        def _():
            forward(nz - 4 - t)

        @pl.when(t + 1 < nz)
        def _():
            need_q(t + 1)

        @pl.when(t + 1 == nz)
        def _():
            len_copy.wait_recv()
            kv[0].wait_recv()
            set_bias(1, plen[0:1, :])

        @pl.when(t == nz)
        def _():
            kv[1].wait_recv()
            turn(1)

    def after(t):
        @pl.when(t >= nz)
        def _():
            send_x(t - nz)

        @pl.when(t >= nz + 1)
        def _():
            send_z(t - nz - 1)

    need_q(0)
    m = None
    for j in range(chunks):
        m = scores(0, z, s_a, j, m)
    m = fresh_scores(0, z, s_a, m)

    def pair(i, m):
        t = 2 * i
        before(t)
        m = step(t, s_a, s_b, m, True)
        after(t)
        before(t + 1)
        m = step(t + 1, s_b, s_a, m, True)
        after(t + 1)
        return m

    m = lax.fori_loop(0, nz - 1, pair, m)
    last = 2 * nz - 2
    before(last)
    m = step(last, s_a, s_b, m, True)
    after(last)
    step(last + 1, s_b, s_a, m, False)
    after(last + 1)

    items = [merge_x(nz - 1)]
    for k in range(nz - 1):
        pz_arrival(k).wait_recv()
        items.append(decode(zin.at[k]))
    value, peak, total, peak_total = merged(items)
    value = value * (jnp.exp2(peak - peak_total) / total)
    fout[...] = value.T.astype(jnp.bfloat16)

    def home(off):
        w, h_, y_ = col_peer(off)
        src = fout.at[pl.ds(pl.multiple_of(w * 16, 16), 16), :]
        return remote(src, fin.at[NY * h + y], f_s.at[w], f_r.at[u], at(h_, x, y_, z))

    def home_arrival(off):
        w, h_, y_ = col_peer(off)
        src = fout.at[pl.ds(0, 16), :]
        return remote(src, fin.at[NY * h_ + y_], f_s.at[w], f_r.at[w], at(h_, x, y_, z))

    for off in range(1, COL):
        home(off).start()
    fin[NY * h + y] = fout[pl.ds(pl.multiple_of(u * 16, 16), 16), :]
    for off in range(1, COL):
        home_arrival(off).wait_recv()
    out[...] = fin[...]

    for off in range(1, COL):
        col_copy(off).wait_send()
        home(off).wait_send()
    len_copy.wait_send()
    for copy in kv:
        copy.wait_send()
    for t in range(nz):
        for off in range(1, nx):
            qx_copy(t, off).wait_send()
            px_copy(t, off).wait_send()
        if t < nz - 1:
            qz_copy(t).wait_send()
            pz_copy(t).wait_send()


def shards(nx, nz, q_new, kv_new, k_cache, v_cache, span_len, order):
    kv_dev, slots, width = k_cache.shape
    tokens = q_new.shape[0]
    kv_heads = NH * kv_dev
    group = q_new.shape[1] // (kv_heads * width)
    rows = 128 * nx
    bf = jnp.bfloat16
    queries = q_new.reshape(tokens, kv_heads * group, width).transpose(1, 0, 2)
    queries = queries.reshape(kv_heads * group * tokens, width)
    fresh = kv_new.reshape(tokens, kv_heads * 2, width).transpose(1, 0, 2)
    fresh = fresh.reshape(kv_heads * 2 * tokens, width)
    places = order.reshape(NH, -1)
    scale2 = width ** (-0.5) * 1.4426950408889634
    vmem = pl.BlockSpec(memory_space=pltpu.VMEM)
    hbm = pl.BlockSpec(memory_space=pltpu.HBM)
    smem = pl.BlockSpec(memory_space=pltpu.SMEM)
    i16 = jnp.int16
    f32 = jnp.float32
    dma = pltpu.SemaphoreType.DMA
    out = pl.pallas_call(
        functools.partial(kernel, nx, nz, scale2),
        out_shape=jax.ShapeDtypeStruct((kv_heads, tokens * group, width), bf),
        in_specs=[hbm, hbm, smem, hbm, hbm, hbm],
        out_specs=vmem,
        scratch_shapes=[
            pltpu.VMEM(queries.shape, bf),
            pltpu.VMEM(fresh.shape, bf),
            pltpu.VMEM(places.shape, jnp.int32),
            pltpu.VMEM((COL, 32, width), bf),
            pltpu.VMEM((nz, 8, rows), f32),
            pltpu.VMEM((8, 128), f32),
            pltpu.VMEM((COL, 32, width), bf),
            pltpu.VMEM((nz, rows, width), bf),
            pltpu.VMEM((2, slots, width), bf),
            pltpu.VMEM((2, slots, width), bf),
            pltpu.VMEM((2, width, slots), bf),
            pltpu.VMEM((2, 16, width), bf),
            pltpu.VMEM((2, 16, width), bf),
            pltpu.VMEM((3, 16, width), f32),
            pltpu.VMEM((2, slots, 128), f32),
            pltpu.VMEM((8, 128), f32),
            pltpu.VMEM((slots + 8, rows), f32),
            pltpu.VMEM((slots + 8, rows), f32),
            pltpu.VMEM((width, rows), f32),
            pltpu.VMEM((nz, nx, width + 8, 128), f32),
            pltpu.VMEM((nz, nx, width + 16, 128), i16),
            pltpu.VMEM((nz, nx, width + 16, 128), i16),
            pltpu.VMEM((nz, width + 16, 128), i16),
            pltpu.VMEM((nz, width + 16, 128), i16),
            pltpu.VMEM((kv_heads, 16, width), bf),
            pltpu.VMEM((128, width), bf),
            dma((COL,)), dma((COL,)), dma, dma, dma((2,)), dma((2,)), dma((5,)),
            dma((nz,)), dma((nz,)), dma((nz, nx)), dma((nz, nx)),
            dma((nz, nx)), dma((nz, nx)), dma((nz,)), dma((nz,)), dma((COL,)), dma((COL,)),
        ],
        compiler_params=pltpu.CompilerParams(
            collective_id=0, has_side_effects=True, vmem_limit_bytes=62 << 20
        ),
    )(queries, fresh, span_len, places, k_cache, v_cache)
    out = out.reshape(kv_heads * group, tokens, width).transpose(1, 0, 2)
    return out.reshape(tokens, kv_heads * group * width)


def solution(mesh):
    nz = 8
    nx = mesh.shape["ctx"] // (nz * NY)
    return jax.shard_map(
        functools.partial(shards, nx, nz),
        mesh=mesh,
        in_specs=(
            P(("head", "ctx"), None),
            P(("head", "ctx"), None),
            P("head", "ctx", None),
            P("head", "ctx", None),
            P("ctx"),
            P(),
        ),
        out_specs=P(("head", "ctx"), None),
        check_vma=False,
    )
```

time: 81.3 us -> 71.7 us (0.88)
  Pallas kernels: 76 us -> 69.4 us
  local copies, waits for them, and re-layouts: 3.51 us -> 1.4 us
  other arithmetic: 0.85 us -> 0 us
    pallas_call x1, Pallas kernels: 76 us -> 69.4 us  [shards(): pl.pallas_call(functools.partial(kernel, nx, nz, scale2), out_shape=jax.S...]
    reshape x2 -> x0, local copies, waits for them, and re-layouts: 0.91 us -> none  [the longest x1 0.77 us: shards(): queries = queries.reshape(kv_heads, tokens * group, width)]
    unnamed x8 -> x1, local copies, waits for them, and re-layouts: 1.88 us -> 1.4 us
where the time goes in v2:
time: 71.7 us; the launch traced here: 71.5 us
  Pallas kernels  69.4 us (97%)
  local copies, waits for them, and re-layouts  1.4 us (2%)
    pallas_call x1, Pallas kernels, shards(): pl.pallas_call(functools.partial(kernel, nx, nz, scale2), out_shape=jax.S...  69.4 us

profile of v2, /device:TPU:1, one launch (start us, length us, event | category | flops | bytes accessed | tf_op | source)
XLA Modules:
  0.0 71.5 jit_solution(11464988592300874244)
XLA Ops:
  0.7 69.4 %shard_map.64 = bf16[8,16,128]{2,1,0:T(8,128)(2,1)} custom-call(bf16[128,128]{1,0:T(8,128)(2,1)} %bitcast.17, bf16[32,128]{1,0:T(8,128)(2,1)} %bitcast.18, s32[1]{0:T(128)S(6)} %copy.11.len_smem, s32[4,128]{1,0:T(4,128)} %bitcast.19, bf16[2,2048,128]{2,1,0:T(8,128)(2,1)} %k_hbm.1, bf16[2,2048,128]{2,1,0:T(8,128)(2,1)} %v_hbm.1), custom_call_target="tpu_custom_call" | custom-call | tf_op jit(solution)/shard_map/pallas_call | solution.py:458
  70.1 1.4 %copy.12 = bf16[2,8192]{1,0:T(2,128)(2,1)} copy(bf16[2,8192]{1,0:T(2,128)(2,1)} %bitcast.16) | data formatting | bytes 65536

commit v3 on v2

--- a/solution.py
+++ b/solution.py
@@ -13,15 +13,16 @@
 NY = 2
 COL = NH * NY
 CHUNK = 256
+LAG = 3
 
 
 def kernel(
     nx, nz, scale2,
-    q_hbm, f_hbm, len_smem, ord_hbm, k_hbm, v_hbm,
+    q_hbm, f_hbm, len_hbm, ord_hbm, k_hbm, v_hbm,
     out,
-    q_in, f_in, ord_in, msg, ordq, lens,
-    col, qall, kb, vb, vt, kf, vf, fresh_f, bias, plen, s_a, s_b, acc, part,
-    xout, xin, zout, zin, fin, fout,
+    q_in, f_in, ord_in, len_smem, msg, ordq, lens,
+    col, qall, kb, vb, vt, vo, kf, vf, fresh_f, bias, plen, s_a, s_b, acc, part,
+    xout, xin, zfull, zout, zin, fout,
     col_s, col_r, len_s, len_r, kv_s, kv_r, own_sem, qz_s, qz_r, qx_s, qx_r,
     px_s, px_r, pz_s, pz_r, f_s, f_r,
 ):
@@ -33,6 +34,7 @@
     u = y * NH + h
     slots = k_hbm.shape[1]
     rows = 128 * nx
+    width = k_hbm.shape[2]
     chunks = slots // CHUNK
 
     def at(h_, x_, y_, z_):
@@ -47,21 +49,23 @@
             src_ref=src, dst_ref=dst, send_sem=ss, recv_sem=rs, device_id=dev, device_id_type=MESH
         )
 
-    def far(t):
-        half = lax.div(t, 2)
-        return jnp.where(lax.rem(t, 2) == 0, nz // 2 + half, nz // 2 - 1 - half)
+    def far(k):
+        half = lax.div(k - 2, 2)
+        rest = jnp.where(lax.rem(k, 2) == 0, nz // 2 + half, nz // 2 - 1 - half)
+        return jnp.where(k == 0, 1, jnp.where(k == 1, nz - 1, jnp.where(k == nz - 1, 0, rest)))
 
     def plane(t):
         return lax.rem(z + far(t), nz)
 
     own = [
         pltpu.make_async_copy(k_hbm.at[y], kb.at[0], own_sem.at[0]),
-        pltpu.make_async_copy(v_hbm.at[y], vb.at[0], own_sem.at[1]),
+        pltpu.make_async_copy(v_hbm, vb, own_sem.at[1]),
     ]
     small = [
         pltpu.make_async_copy(q_hbm, q_in, own_sem.at[2]),
         pltpu.make_async_copy(f_hbm, f_in, own_sem.at[3]),
         pltpu.make_async_copy(ord_hbm, ord_in, own_sem.at[4]),
+        pltpu.make_async_copy(len_hbm, len_smem, own_sem.at[5]),
     ]
     for copy in small + own:
         copy.start()
@@ -75,12 +79,14 @@
             barrier, inc=1, device_id=at(h, x, y, lax.rem(z + off, nz)), device_id_type=MESH
         )
     for off in range(1, nx):
-        pl.semaphore_signal(
-            barrier, inc=1, device_id=at(h, lax.rem(x + off, nx), y, z), device_id_type=MESH
-        )
+        for side in (0, 1, nz - 1):
+            to = at(h, lax.rem(x + off, nx), y, lax.rem(z + side, nz))
+            pl.semaphore_signal(barrier, inc=1, device_id=to, device_id_type=MESH)
 
     tile_row = lax.broadcasted_iota(jnp.int32, (8, 128), 0)
-    pair_row = lax.broadcasted_iota(jnp.int32, (16, 128), 0)
+    wide_row = lax.broadcasted_iota(jnp.int32, (8, rows), 0)
+    for copy in small:
+        copy.wait()
     lens[...] = jnp.zeros((8, 128), jnp.float32) + len_smem[0].astype(jnp.float32)
 
     def set_bias(span, length):
@@ -89,12 +95,6 @@
             bias[span, j * CHUNK : (j + 1) * CHUNK, :] = jnp.where(slot < length, 0.0, masked)
 
     set_bias(0, lens[0:1, :])
-    for d in range(nz):
-        for w in range(nx):
-            part[d, w, 0:128, :] = jnp.zeros((128, 128), jnp.float32)
-            part[d, w, 128:136, :] = jnp.where(tile_row == 0, masked, 0.0)
-    for copy in small:
-        copy.wait()
     for w in range(COL):
         msg[w, 0:16, :] = q_in[w * 16 : (w + 1) * 16, :]
         msg[w, 16:32, :] = f_in[w // 4 * 16 : w // 4 * 16 + 16, :]
@@ -116,7 +116,14 @@
         )
         ordq[d] = jnp.broadcast_to(jnp.sum(both, axis=0, keepdims=True), (8, rows))
 
-    pl.semaphore_wait(barrier, COL + nz + nx - 3)
+    for copy in own:
+        copy.wait()
+    for j in range(slots // 128):
+        cut = slice(j * 128, (j + 1) * 128)
+        vt[0, :, cut] = vb[y, cut, :].T
+        vo[:, cut] = vb[1 - y, cut, :].T
+
+    pl.semaphore_wait(barrier, COL + nz - 2 + 3 * (nx - 1))
 
     def col_copy(off):
         w, h_, y_ = col_peer(off)
@@ -135,19 +142,12 @@
     len_copy.start()
     kv = [
         remote(k_hbm.at[1 - y], kb.at[1], kv_s.at[0], kv_r.at[0], partner),
-        remote(v_hbm.at[1 - y], vb.at[1], kv_s.at[1], kv_r.at[1], partner),
+        remote(vo, vt.at[1], kv_s.at[1], kv_r.at[1], partner),
     ]
     for copy in kv:
         copy.start()
     col[u] = msg[NY * h + y]
 
-    def turn(span):
-        for j in range(slots // 128):
-            vt[span, :, j * 128 : (j + 1) * 128] = vb[span, j * 128 : (j + 1) * 128, :].T
-
-    for copy in own:
-        copy.wait()
-    turn(0)
     for off in range(1, COL):
         col_arrival(off).wait_recv()
 
@@ -160,6 +160,11 @@
         ref = qall.at[z, pl.ds(base, 128), :]
         return remote(ref, ref, qz_s.at[t], qz_r.at[t], at(h, x, y, to))
 
+    def qd_copy(k, off):
+        to = lax.rem(z + nz - far(k), nz)
+        ref = qall.at[z, pl.ds(base, 128), :]
+        return remote(ref, ref, qx_s.at[k, off], qx_r.at[k, off], at(h, lax.rem(x + off, nx), y, to))
+
     def qz_arrival(t):
         ref = qall.at[plane(t), pl.ds(base, 128), :]
         return remote(ref, ref, qz_s.at[t], qz_r.at[t], at(h, x, y, plane(t)))
@@ -177,7 +182,10 @@
 
     for off in range(1, nx):
         qx_copy(nz - 1, off).start()
-    for k in reversed(range(nz - 1)):
+    for k in range(2):
+        for off in range(nx):
+            qd_copy(k, off).start()
+    for k in reversed(range(2, nz - 1)):
         qz_copy(k).start()
 
     for span in range(2):
@@ -206,9 +214,6 @@
         for off in range(1, nx):
             qx_copy(k, off).start()
 
-    for t in range(1, min(3, nz)):
-        forward(nz - 1 - t)
-
     def scores(span, d, s_ref, j, m):
         keys = kb[span, j * CHUNK : (j + 1) * CHUNK, :]
         s = lax.dot_general(
@@ -247,23 +252,71 @@
         )
         return total + p
 
-    def add_part(d, peak, total):
+    def keep_part(d, peak, total):
         total = jnp.sum(total, axis=0, keepdims=True)
+        part[d, 0:width, :] = acc[...]
+        part[d, width : width + 8, :] = jnp.where(wide_row == 0, peak, total)
+
+    def whole_part(d, peak, total):
+        total = jnp.sum(total, axis=0, keepdims=True)
+        old = part[d, width : width + 8, :]
+        new_peak = jnp.maximum(old[0:1, :], peak)
+        keep = jnp.exp2(old[0:1, :] - new_peak)
+        take = jnp.exp2(peak - new_peak)
+        value = part[d, 0:width, :] * keep + acc[...] * take
+        return value, new_peak, old[1:2, :] * keep + total * take, new_peak
+
+    def encode(value, peak, total, peak_total):
+        size = jnp.maximum(jnp.max(jnp.abs(value), axis=0, keepdims=True), 1e-30)
+        power = jnp.ceil(jnp.log2(size) + peak + 1e-3) - 15.0
+        power_t = jnp.ceil(jnp.log2(total) + peak_total + 1e-3) - 15.0
+        units = value * jnp.exp2(peak - power)
+        units = (units + 12582912.0) - 12582912.0
+        whole = total * jnp.exp2(peak_total - power_t)
+        high = jnp.floor(whole)
+        low = jnp.floor((whole - high) * 32767.0)
+        row = lax.broadcasted_iota(jnp.int32, (16, value.shape[1]), 0)
+        tail = jnp.where(row == 0, power, jnp.where(row == 1, power_t, high))
+        tail = jnp.where(row == 3, low, tail)
+        both = [item.astype(jnp.int32).astype(jnp.int16) for item in (units, tail)]
+        return both
+
+    def decode(ref):
+        tail = ref[width : width + 16, :].astype(jnp.int32).astype(jnp.float32)
+        total = tail[2:3, :] + tail[3:4, :] * (1.0 / 32767.0)
+        value = ref[0:width, :].astype(jnp.int32).astype(jnp.float32)
+        return value, tail[0:1, :], total, tail[1:2, :]
+
+    def merged(items):
+        peak = functools.reduce(jnp.maximum, [item[1] for item in items])
+        peak_total = functools.reduce(jnp.maximum, [item[3] for item in items])
+        value = sum(item[0] * jnp.exp2(item[1] - peak) for item in items)
+        total = sum(item[2] * jnp.exp2(item[3] - peak_total) for item in items)
+        return value, peak, total, peak_total
+
+    def put_part(k, item):
+        units, tail = encode(*item)
         for w in range(nx):
-            cut = slice(w * 128, (w + 1) * 128)
-            old = part[d, w, 128:136, :]
-            new_peak = jnp.maximum(old[0:1, :], peak[:, cut])
-            keep = jnp.exp2(old[0:1, :] - new_peak)
-            take = jnp.exp2(peak[:, cut] - new_peak)
-            part[d, w, 0:128, :] = part[d, w, 0:128, :] * keep + acc[:, cut] * take
-            new_total = old[1:2, :] * keep + total[:, cut] * take
-            part[d, w, 128:136, :] = jnp.where(tile_row == 0, new_peak, new_total)
+            side = slice(w * 128, (w + 1) * 128)
+            xout[k, w, 0:width, :] = units[:, side]
+            xout[k, w, width : width + 16, :] = tail[:, side]
+
+    def put_own_part(item):
+        for w in range(nx):
+            side = slice(w * 128, (w + 1) * 128)
+            items = [tuple(array[:, side] for array in item)]
+            items += [decode(zfull.at[k, w]) for k in range(2)]
+            units, tail = encode(*merged(items))
+            xout[nz - 1, w, 0:width, :] = units
+            xout[nz - 1, w, width : width + 16, :] = tail
 
     def order_of(t):
-        return jnp.where(t < nz, nz - 1 - t, t - nz)
-
-    def step(t, s_now, s_next, m, ahead):
-        span, d = lax.div(t, nz), plane(order_of(t))
+        first = jnp.where(t == 0, nz - 1, jnp.where(t < 3, t - 1, nz + 1 - t))
+        return jnp.where(t < nz, first, t - nz)
+
+    def step(t, span, s_now, s_next, m, ahead=True, own_plane=False):
+        k = order_of(t)
+        d = plane(k)
         span_n, d_n = lax.div(t + 1, nz), plane(order_of(t + 1))
         peak = jnp.max(m, axis=0, keepdims=True) * scale2
         total = jnp.zeros((8, rows), jnp.float32)
@@ -275,42 +328,30 @@
         if ahead:
             nxt = fresh_scores(span_n, d_n, s_next, nxt)
         total = fresh_weights(span, s_now, peak, total)
-        add_part(d, peak, total)
+        if span == 0:
+            keep_part(d, peak, total)
+        elif own_plane:
+            for j in range(2):
+                pf_arrival(j).wait_recv()
+            put_own_part(whole_part(d, peak, total))
+        else:
+            put_part(k, whole_part(d, peak, total))
         return nxt
-
-    def encode(ref, value, peak, total, peak_total):
-        size = jnp.maximum(jnp.max(jnp.abs(value), axis=0, keepdims=True), 1e-30)
-        power = jnp.ceil(jnp.log2(size) + peak + 1e-3) - 15.0
-        power_t = jnp.ceil(jnp.log2(total) + peak_total + 1e-3) - 15.0
-        units = value * jnp.exp2(peak - power)
-        units = (units + 12582912.0) - 12582912.0
-        whole = total * jnp.exp2(peak_total - power_t)
-        high = jnp.floor(whole)
-        low = jnp.floor((whole - high) * 32767.0)
-        tail = jnp.where(pair_row == 0, power, jnp.where(pair_row == 1, power_t, high))
-        tail = jnp.where(pair_row == 3, low, tail)
-        ref[0:128, :] = units.astype(jnp.int32).astype(jnp.int16)
-        ref[128:144, :] = tail.astype(jnp.int32).astype(jnp.int16)
-
-    def decode(ref):
-        tail = ref[128:144, :].astype(jnp.int32).astype(jnp.float32)
-        total = tail[2:3, :] + tail[3:4, :] * (1.0 / 32767.0)
-        return ref[0:128, :].astype(jnp.int32).astype(jnp.float32), tail[0:1, :], total, tail[1:2, :]
-
-    def merged(items):
-        peak = functools.reduce(jnp.maximum, [item[1] for item in items])
-        peak_total = functools.reduce(jnp.maximum, [item[3] for item in items])
-        value = sum(item[0] * jnp.exp2(item[1] - peak) for item in items)
-        total = sum(item[2] * jnp.exp2(item[3] - peak_total) for item in items)
-        return value, peak, total, peak_total
 
     def px_copy(k, off):
         who = lax.rem(x + off, nx)
-        return remote(xout.at[k, off], xin.at[k, off], px_s.at[k, off], px_r.at[k, off], at(h, who, y, z))
+        return remote(xout.at[k, who], xin.at[k, off], px_s.at[k, off], px_r.at[k, off], at(h, who, y, z))
 
     def px_arrival(k, off):
         who = lax.rem(x + nx - off, nx)
-        return remote(xout.at[k, off], xin.at[k, off], px_s.at[k, off], px_r.at[k, off], at(h, who, y, z))
+        return remote(xout.at[k, who], xin.at[k, off], px_s.at[k, off], px_r.at[k, off], at(h, who, y, z))
+
+    def pf_copy(k):
+        return remote(xout.at[k], zfull.at[k], pz_s.at[k], pz_r.at[k], at(h, x, y, plane(k)))
+
+    def pf_arrival(k):
+        who = lax.rem(z + nz - far(k), nz)
+        return remote(xout.at[k], zfull.at[k], pz_s.at[k], pz_r.at[k], at(h, x, y, who))
 
     def pz_copy(k):
         return remote(zout.at[k], zin.at[k], pz_s.at[k], pz_r.at[k], at(h, x, y, plane(k)))
@@ -320,37 +361,38 @@
         return remote(zout.at[k], zin.at[k], pz_s.at[k], pz_r.at[k], at(h, x, y, who))
 
     def send_x(k):
-        d = plane(k)
         for off in range(1, nx):
-            who = lax.rem(x + off, nx)
-            tile = part[d, who, 128:136, :]
-            encode(xout.at[k, off], part[d, who, 0:128, :], tile[0:1, :], tile[1:2, :], tile[0:1, :])
             px_copy(k, off).start()
 
     def merge_x(k):
-        tile = part[plane(k), x, 128:136, :]
-        items = [(part[plane(k), x, 0:128, :], tile[0:1, :], tile[1:2, :], tile[0:1, :])]
+        items = [decode(xout.at[k, x])]
         for off in range(1, nx):
             px_arrival(k, off).wait_recv()
-            items.append(decode(xin.at[k, off]))
+        items += [decode(xin.at[k, off]) for off in range(1, nx)]
         return merged(items)
 
     def send_z(k):
-        encode(zout.at[k], *merge_x(k))
+        units, tail = encode(*merge_x(k))
+        zout[k, 0:width, :] = units
+        zout[k, width : width + 16, :] = tail
         pz_copy(k).start()
 
-    def need_q(t):
+    def need_x(k):
         for off in range(1, nx):
-            qx_arrival(nz - 1 - t, off).wait_recv()
+            qx_arrival(k, off).wait_recv()
 
     def before(t):
-        @pl.when(t + 3 < nz)
-        def _():
-            forward(nz - 4 - t)
+        @pl.when(t + 5 < nz)
+        def _():
+            forward(nz + 1 - (t + 5))
 
         @pl.when(t + 1 < nz)
         def _():
-            need_q(t + 1)
+            need_x(order_of(t + 1))
+
+        @pl.when(t + 1 < 3)
+        def _():
+            qx_arrival(order_of(t + 1), 0).wait_recv()
 
         @pl.when(t + 1 == nz)
         def _():
@@ -358,46 +400,55 @@
             kv[0].wait_recv()
             set_bias(1, plen[0:1, :])
 
-        @pl.when(t == nz)
-        def _():
-            kv[1].wait_recv()
-            turn(1)
-
-    def after(t):
-        @pl.when(t >= nz)
-        def _():
-            send_x(t - nz)
-
-        @pl.when(t >= nz + 1)
-        def _():
-            send_z(t - nz - 1)
-
-    need_q(0)
+    def after(k):
+        @pl.when(k < 2)
+        def _():
+            pf_copy(k).start()
+
+        @pl.when(k >= 2)
+        def _():
+            send_x(k)
+
+        @pl.when(k >= 2 + LAG)
+        def _():
+            send_z(k - LAG)
+
+    need_x(nz - 1)
     m = None
     for j in range(chunks):
         m = scores(0, z, s_a, j, m)
     m = fresh_scores(0, z, s_a, m)
-
-    def pair(i, m):
+    for t in range(3, min(5, nz)):
+        forward(nz + 1 - t)
+
+    def pair0(i, m):
         t = 2 * i
         before(t)
-        m = step(t, s_a, s_b, m, True)
-        after(t)
+        m = step(t, 0, s_a, s_b, m)
         before(t + 1)
-        m = step(t + 1, s_b, s_a, m, True)
-        after(t + 1)
+        return step(t + 1, 0, s_b, s_a, m)
+
+    m = lax.fori_loop(0, nz // 2, pair0, m)
+    kv[1].wait_recv()
+
+    def pair1(i, m):
+        k = 2 * i
+        m = step(nz + k, 1, s_a, s_b, m)
+        after(k)
+        m = step(nz + k + 1, 1, s_b, s_a, m)
+        after(k + 1)
         return m
 
-    m = lax.fori_loop(0, nz - 1, pair, m)
-    last = 2 * nz - 2
-    before(last)
-    m = step(last, s_a, s_b, m, True)
-    after(last)
-    step(last + 1, s_b, s_a, m, False)
-    after(last + 1)
+    m = lax.fori_loop(0, nz // 2 - 1, pair1, m)
+    m = step(2 * nz - 2, 1, s_a, s_b, m)
+    after(nz - 2)
+    step(2 * nz - 1, 1, s_b, s_a, m, ahead=False, own_plane=True)
+    after(nz - 1)
+    for k in range(max(nz - LAG, 2), nz - 1):
+        send_z(k)
 
     items = [merge_x(nz - 1)]
-    for k in range(nz - 1):
+    for k in range(2, nz - 1):
         pz_arrival(k).wait_recv()
         items.append(decode(zin.at[k]))
     value, peak, total, peak_total = merged(items)
@@ -407,33 +458,42 @@
     def home(off):
         w, h_, y_ = col_peer(off)
         src = fout.at[pl.ds(pl.multiple_of(w * 16, 16), 16), :]
-        return remote(src, fin.at[NY * h + y], f_s.at[w], f_r.at[u], at(h_, x, y_, z))
+        return remote(src, out.at[NY * h + y], f_s.at[w], f_r.at[u], at(h_, x, y_, z))
 
     def home_arrival(off):
         w, h_, y_ = col_peer(off)
         src = fout.at[pl.ds(0, 16), :]
-        return remote(src, fin.at[NY * h_ + y_], f_s.at[w], f_r.at[w], at(h_, x, y_, z))
+        return remote(src, out.at[NY * h_ + y_], f_s.at[w], f_r.at[w], at(h_, x, y_, z))
 
     for off in range(1, COL):
         home(off).start()
-    fin[NY * h + y] = fout[pl.ds(pl.multiple_of(u * 16, 16), 16), :]
-    for off in range(1, COL):
-        home_arrival(off).wait_recv()
-    out[...] = fin[...]
+    rest = pltpu.make_async_copy(
+        fout.at[pl.ds(pl.multiple_of(u * 16, 16), 16), :], out.at[NY * h + y], own_sem.at[0]
+    )
+    rest.start()
 
     for off in range(1, COL):
         col_copy(off).wait_send()
-        home(off).wait_send()
     len_copy.wait_send()
     for copy in kv:
         copy.wait_send()
-    for t in range(nz):
-        for off in range(1, nx):
-            qx_copy(t, off).wait_send()
-            px_copy(t, off).wait_send()
-        if t < nz - 1:
-            qz_copy(t).wait_send()
-            pz_copy(t).wait_send()
+    for k in range(nz):
+        if k >= 2:
+            for off in range(1, nx):
+                qx_copy(k, off).wait_send()
+                px_copy(k, off).wait_send()
+        if k < 2:
+            for off in range(nx):
+                qd_copy(k, off).wait_send()
+            pf_copy(k).wait_send()
+        elif k < nz - 1:
+            qz_copy(k).wait_send()
+            pz_copy(k).wait_send()
+    for off in range(1, COL):
+        home_arrival(off).wait_recv()
+    rest.wait()
+    for off in range(1, COL):
+        home(off).wait_send()
 
 
 def shards(nx, nz, q_new, kv_new, k_cache, v_cache, span_len, order):
@@ -451,19 +511,19 @@
     scale2 = width ** (-0.5) * 1.4426950408889634
     vmem = pl.BlockSpec(memory_space=pltpu.VMEM)
     hbm = pl.BlockSpec(memory_space=pltpu.HBM)
-    smem = pl.BlockSpec(memory_space=pltpu.SMEM)
     i16 = jnp.int16
     f32 = jnp.float32
     dma = pltpu.SemaphoreType.DMA
     out = pl.pallas_call(
         functools.partial(kernel, nx, nz, scale2),
         out_shape=jax.ShapeDtypeStruct((kv_heads, tokens * group, width), bf),
-        in_specs=[hbm, hbm, smem, hbm, hbm, hbm],
-        out_specs=vmem,
+        in_specs=[hbm] * 6,
+        out_specs=hbm,
         scratch_shapes=[
             pltpu.VMEM(queries.shape, bf),
             pltpu.VMEM(fresh.shape, bf),
             pltpu.VMEM(places.shape, jnp.int32),
+            pltpu.SMEM(span_len.shape, jnp.int32),
             pltpu.VMEM((COL, 32, width), bf),
             pltpu.VMEM((nz, 8, rows), f32),
             pltpu.VMEM((8, 128), f32),
@@ -472,6 +532,7 @@
             pltpu.VMEM((2, slots, width), bf),
             pltpu.VMEM((2, slots, width), bf),
             pltpu.VMEM((2, width, slots), bf),
+            pltpu.VMEM((width, slots), bf),
             pltpu.VMEM((2, 16, width), bf),
             pltpu.VMEM((2, 16, width), bf),
             pltpu.VMEM((3, 16, width), f32),
@@ -480,14 +541,14 @@
             pltpu.VMEM((slots + 8, rows), f32),
             pltpu.VMEM((slots + 8, rows), f32),
             pltpu.VMEM((width, rows), f32),
-            pltpu.VMEM((nz, nx, width + 8, 128), f32),
+            pltpu.VMEM((nz, width + 8, rows), f32),
             pltpu.VMEM((nz, nx, width + 16, 128), i16),
             pltpu.VMEM((nz, nx, width + 16, 128), i16),
+            pltpu.VMEM((2, nx, width + 16, 128), i16),
             pltpu.VMEM((nz, width + 16, 128), i16),
             pltpu.VMEM((nz, width + 16, 128), i16),
-            pltpu.VMEM((kv_heads, 16, width), bf),
             pltpu.VMEM((128, width), bf),
-            dma((COL,)), dma((COL,)), dma, dma, dma((2,)), dma((2,)), dma((5,)),
+            dma((COL,)), dma((COL,)), dma, dma, dma((2,)), dma((2,)), dma((6,)),
             dma((nz,)), dma((nz,)), dma((nz, nx)), dma((nz, nx)),
             dma((nz, nx)), dma((nz, nx)), dma((nz,)), dma((nz,)), dma((COL,)), dma((COL,)),
         ],

time: 71.7 us -> 62.9 us (0.88)
  Pallas kernels: 69.4 us -> 60.6 us
    pallas_call x1, Pallas kernels: 69.4 us -> 60.6 us  [shards(): pl.pallas_call(functools.partial(kernel, nx, nz, scale2), out_shape=jax.S...]
where the time goes in v3:
time: 62.9 us; the launch traced here: 62.7 us
  Pallas kernels  60.6 us (96%)
  local copies, waits for them, and re-layouts  1.4 us (2%)
  between operations  0.66 us (1%)
    pallas_call x1, Pallas kernels, shards(): pl.pallas_call(functools.partial(kernel, nx, nz, scale2), out_shape=jax.S...  60.6 us
    unnamed x1, local copies, waits for them, and re-layouts  1.4 us

profile of v3, /device:TPU:1, one launch (start us, length us, event | category | flops | bytes accessed | tf_op | source)
XLA Modules:
  0.0 62.7 jit_solution(7624874948661390965)
XLA Ops:
  0.7 60.6 %shard_map.64 = bf16[8,16,128]{2,1,0:T(8,128)(2,1)} custom-call(bf16[128,128]{1,0:T(8,128)(2,1)} %bitcast.17, bf16[32,128]{1,0:T(8,128)(2,1)} %bitcast.18, s32[1]{0:T(128)S(6)} %copy.11.len_hbm, s32[4,128]{1,0:T(4,128)} %bitcast.19, bf16[2,2048,128]{2,1,0:T(8,128)(2,1)} %k_hbm.1, bf16[2,2048,128]{2,1,0:T(8,128)(2,1)} %v_hbm.1), custom_call_target="tpu_custom_call" | custom-call | tf_op jit(solution)/shard_map/pallas_call | solution.py:517
  61.3 1.4 %copy.12 = bf16[2,8192]{1,0:T(2,128)(2,1)} copy(bf16[2,8192]{1,0:T(2,128)(2,1)} %bitcast.16) | data formatting | bytes 65536

commit v4 on v3

--- a/solution.py
+++ b/solution.py
@@ -12,6 +12,7 @@
 NH = 4
 NY = 2
 COL = NH * NY
+FAR_FIRST = (2, 6, 3, 5, 1, 7, 4)
 CHUNK = 256
 LAG = 3
 
@@ -79,9 +80,9 @@
             barrier, inc=1, device_id=at(h, x, y, lax.rem(z + off, nz)), device_id_type=MESH
         )
     for off in range(1, nx):
-        for side in (0, 1, nz - 1):
-            to = at(h, lax.rem(x + off, nx), y, lax.rem(z + side, nz))
-            pl.semaphore_signal(barrier, inc=1, device_id=to, device_id_type=MESH)
+        pl.semaphore_signal(
+            barrier, inc=1, device_id=at(h, lax.rem(x + off, nx), y, z), device_id_type=MESH
+        )
 
     tile_row = lax.broadcasted_iota(jnp.int32, (8, 128), 0)
     wide_row = lax.broadcasted_iota(jnp.int32, (8, rows), 0)
@@ -123,7 +124,7 @@
         vt[0, :, cut] = vb[y, cut, :].T
         vo[:, cut] = vb[1 - y, cut, :].T
 
-    pl.semaphore_wait(barrier, COL + nz - 2 + 3 * (nx - 1))
+    pl.semaphore_wait(barrier, COL + nz + nx - 3)
 
     def col_copy(off):
         w, h_, y_ = col_peer(off)
@@ -135,7 +136,7 @@
         w, h_, y_ = col_peer(off)
         return remote(msg.at[0], col.at[w], col_s.at[w], col_r.at[w], at(h_, x, y_, z))
 
-    for off in range(1, COL):
+    for off in FAR_FIRST:
         col_copy(off).start()
     partner = at(h, x, 1 - y, z)
     len_copy = remote(lens, plen, len_s, len_r, partner)
@@ -160,10 +161,13 @@
         ref = qall.at[z, pl.ds(base, 128), :]
         return remote(ref, ref, qz_s.at[t], qz_r.at[t], at(h, x, y, to))
 
-    def qd_copy(k, off):
+    def qf_copy(k):
         to = lax.rem(z + nz - far(k), nz)
-        ref = qall.at[z, pl.ds(base, 128), :]
-        return remote(ref, ref, qx_s.at[k, off], qx_r.at[k, off], at(h, lax.rem(x + off, nx), y, to))
+        return remote(qall.at[z], qall.at[z], qz_s.at[k], qz_r.at[k], at(h, x, y, to))
+
+    def qf_arrival(k):
+        ref = qall.at[plane(k)]
+        return remote(ref, ref, qz_s.at[k], qz_r.at[k], at(h, x, y, plane(k)))
 
     def qz_arrival(t):
         ref = qall.at[plane(t), pl.ds(base, 128), :]
@@ -182,9 +186,6 @@
 
     for off in range(1, nx):
         qx_copy(nz - 1, off).start()
-    for k in range(2):
-        for off in range(nx):
-            qd_copy(k, off).start()
     for k in reversed(range(2, nz - 1)):
         qz_copy(k).start()
 
@@ -311,7 +312,7 @@
             xout[nz - 1, w, width : width + 16, :] = tail
 
     def order_of(t):
-        first = jnp.where(t == 0, nz - 1, jnp.where(t < 3, t - 1, nz + 1 - t))
+        first = jnp.where(t <= nz - 3, nz - 1 - t, t - (nz - 2))
         return jnp.where(t < nz, first, t - nz)
 
     def step(t, span, s_now, s_next, m, ahead=True, own_plane=False):
@@ -382,17 +383,17 @@
             qx_arrival(k, off).wait_recv()
 
     def before(t):
-        @pl.when(t + 5 < nz)
-        def _():
-            forward(nz + 1 - (t + 5))
-
-        @pl.when(t + 1 < nz)
-        def _():
-            need_x(order_of(t + 1))
-
-        @pl.when(t + 1 < 3)
-        def _():
-            qx_arrival(order_of(t + 1), 0).wait_recv()
+        @pl.when(t + 4 <= nz - 3)
+        def _():
+            forward(nz - 5 - t)
+
+        @pl.when(t + 1 <= nz - 3)
+        def _():
+            need_x(nz - 2 - t)
+
+        @pl.when((t + 1 > nz - 3) & (t + 1 < nz))
+        def _():
+            qf_arrival(t + 1 - (nz - 2)).wait_recv()
 
         @pl.when(t + 1 == nz)
         def _():
@@ -414,12 +415,14 @@
             send_z(k - LAG)
 
     need_x(nz - 1)
+    for k in range(2):
+        qf_copy(k).start()
     m = None
     for j in range(chunks):
         m = scores(0, z, s_a, j, m)
     m = fresh_scores(0, z, s_a, m)
-    for t in range(3, min(5, nz)):
-        forward(nz + 1 - t)
+    for t in range(1, min(4, nz - 2)):
+        forward(nz - 1 - t)
 
     def pair0(i, m):
         t = 2 * i
@@ -429,7 +432,16 @@
         return step(t + 1, 0, s_b, s_a, m)
 
     m = lax.fori_loop(0, nz // 2, pair0, m)
+
+    ahead = None
+    for j in range(chunks):
+        ahead = scores(1, plane(1), s_b, j, ahead)
+    ahead = fresh_scores(1, plane(1), s_b, ahead)
     kv[1].wait_recv()
+    step(nz, 1, s_a, s_b, m, ahead=False)
+    after(0)
+    m = step(nz + 1, 1, s_b, s_a, ahead)
+    after(1)
 
     def pair1(i, m):
         k = 2 * i
@@ -439,7 +451,7 @@
         after(k + 1)
         return m
 
-    m = lax.fori_loop(0, nz // 2 - 1, pair1, m)
+    m = lax.fori_loop(1, nz // 2 - 1, pair1, m)
     m = step(2 * nz - 2, 1, s_a, s_b, m)
     after(nz - 2)
     step(2 * nz - 1, 1, s_b, s_a, m, ahead=False, own_plane=True)
@@ -465,7 +477,7 @@
         src = fout.at[pl.ds(0, 16), :]
         return remote(src, out.at[NY * h_ + y_], f_s.at[w], f_r.at[w], at(h_, x, y_, z))
 
-    for off in range(1, COL):
+    for off in FAR_FIRST:
         home(off).start()
     rest = pltpu.make_async_copy(
         fout.at[pl.ds(pl.multiple_of(u * 16, 16), 16), :], out.at[NY * h + y], own_sem.at[0]
@@ -483,8 +495,7 @@
                 qx_copy(k, off).wait_send()
                 px_copy(k, off).wait_send()
         if k < 2:
-            for off in range(nx):
-                qd_copy(k, off).wait_send()
+            qf_copy(k).wait_send()
             pf_copy(k).wait_send()
         elif k < nz - 1:
             qz_copy(k).wait_send()
@@ -509,7 +520,6 @@
     fresh = fresh.reshape(kv_heads * 2 * tokens, width)
     places = order.reshape(NH, -1)
     scale2 = width ** (-0.5) * 1.4426950408889634
-    vmem = pl.BlockSpec(memory_space=pltpu.VMEM)
     hbm = pl.BlockSpec(memory_space=pltpu.HBM)
     i16 = jnp.int16
     f32 = jnp.float32

time: 62.9 us -> 62.2 us (0.989)
  Pallas kernels: 60.6 us -> 59.9 us
    pallas_call x1, Pallas kernels: 60.6 us -> 59.9 us  [shards(): pl.pallas_call(functools.partial(kernel, nx, nz, scale2), out_shape=jax.S...]
where the time goes in v4:
time: 62.2 us; the launch traced here: 62 us
  Pallas kernels  59.9 us (96%)
  local copies, waits for them, and re-layouts  1.4 us (2%)
  between operations  0.66 us (1%)
    pallas_call x1, Pallas kernels, shards(): pl.pallas_call(functools.partial(kernel, nx, nz, scale2), out_shape=jax.S...  59.9 us
    unnamed x1, local copies, waits for them, and re-layouts  1.4 us

profile of v4, /device:TPU:1, one launch (start us, length us, event | category | flops | bytes accessed | tf_op | source)
XLA Modules:
  0.0 62.0 jit_solution(12830913612813062370)
XLA Ops:
  0.7 59.9 %shard_map.64 = bf16[8,16,128]{2,1,0:T(8,128)(2,1)} custom-call(bf16[128,128]{1,0:T(8,128)(2,1)} %bitcast.17, bf16[32,128]{1,0:T(8,128)(2,1)} %bitcast.18, s32[1]{0:T(128)S(6)} %copy.11.len_hbm, s32[4,128]{1,0:T(4,128)} %bitcast.19, bf16[2,2048,128]{2,1,0:T(8,128)(2,1)} %k_hbm.1, bf16[2,2048,128]{2,1,0:T(8,128)(2,1)} %v_hbm.1), custom_call_target="tpu_custom_call" | custom-call | tf_op jit(solution)/shard_map/pallas_call | solution.py:527
  60.6 1.4 %copy.12 = bf16[2,8192]{1,0:T(2,128)(2,1)} copy(bf16[2,8192]{1,0:T(2,128)(2,1)} %bitcast.16) | data formatting | bytes 65536

commit v5 on v4

--- a/solution.py
+++ b/solution.py
@@ -460,9 +460,12 @@
         send_z(k)
 
     items = [merge_x(nz - 1)]
-    for k in range(2, nz - 1):
+    for k in range(2, nz - 2):
         pz_arrival(k).wait_recv()
         items.append(decode(zin.at[k]))
+    items = [merged(items)]
+    pz_arrival(nz - 2).wait_recv()
+    items.append(decode(zin.at[nz - 2]))
     value, peak, total, peak_total = merged(items)
     value = value * (jnp.exp2(peak - peak_total) / total)
     fout[...] = value.T.astype(jnp.bfloat16)

time: 62.2 us -> 62.2 us (level)
  no operation moved by 1% of the time
where the time goes in v5:
time: 62.2 us; the launch traced here: 62 us
  Pallas kernels  59.9 us (96%)
  local copies, waits for them, and re-layouts  1.4 us (2%)
  between operations  0.66 us (1%)
    pallas_call x1, Pallas kernels, shards(): pl.pallas_call(functools.partial(kernel, nx, nz, scale2), out_shape=jax.S...  59.9 us
    unnamed x1, local copies, waits for them, and re-layouts  1.4 us

profile of v5, /device:TPU:1, one launch (start us, length us, event | category | flops | bytes accessed | tf_op | source)
XLA Modules:
  0.0 62.0 jit_solution(6196431074198460117)
XLA Ops:
  0.7 59.9 %shard_map.64 = bf16[8,16,128]{2,1,0:T(8,128)(2,1)} custom-call(bf16[128,128]{1,0:T(8,128)(2,1)} %bitcast.17, bf16[32,128]{1,0:T(8,128)(2,1)} %bitcast.18, s32[1]{0:T(128)S(6)} %copy.11.len_hbm, s32[4,128]{1,0:T(4,128)} %bitcast.19, bf16[2,2048,128]{2,1,0:T(8,128)(2,1)} %k_hbm.1, bf16[2,2048,128]{2,1,0:T(8,128)(2,1)} %v_hbm.1), custom_call_target="tpu_custom_call" | custom-call | tf_op jit(solution)/shard_map/pallas_call | solution.py:530
  60.6 1.4 %copy.12 = bf16[2,8192]{1,0:T(2,128)(2,1)} copy(bf16[2,8192]{1,0:T(2,128)(2,1)} %bitcast.16) | data formatting | bytes 65536
